TPU v7x, 128 devices: a whole 4x4x4 slice. The times are simulated.
128 devices in a mesh: wide: 32 (over x, y, core), narrow: 4 (over z).
Axes of the slice: x: 4, y: 4, z: 4, core: 2. Of those that a mesh axis runs over, the one named last changes fastest.
Arguments:
- student_hidden: bfloat16 [512, 4096], P(('wide', 'narrow'))
- teacher_hidden: bfloat16 [512, 4096], P(('wide', 'narrow'))
- student_head: bfloat16 [4096, 147456], P(None, ('wide', 'narrow')), may hold values from -0.09375 to 0.09375
- teacher_head: bfloat16 [4096, 147456], P(None, ('wide', 'narrow')), may hold values from -0.09375 to 0.09375
- group_counts: int32 [32], replicated, may hold values from 8 to 16, as said below
- group_offsets: int32 [32], replicated, may hold values from 0 to 496, as said below
Outputs:
- token_kl: float32 [512], P(('wide', 'narrow'))
- hidden_grad: bfloat16 [512, 4096], P(('wide', 'narrow'))
Inputs may be any that keep to these rules, and one draw needn't show every extreme that they name: Group g owns the 16 consecutive token slots from g * 16; its first group_counts[g] slots are live, and some group is full in every draw. The teacher row spans [group_offsets[g], group_offsets[g] + group_counts[g]) of the groups are disjoint and lie inside the 512 rows.
All inputs are finite; a program needn't handle non-finite values.
Results may differ from a plain program's by a relative error of at most 0.0047.
Values may be sent and summed in bfloat16 or wider, within the bound.
A program may use at most 128 MiB of HBM per device.

v0:
```python
import jax
import jax.numpy as jnp
from jax import lax
from jax.sharding import PartitionSpec as P


def shards(student_hidden, teacher_hidden, student_head, teacher_head, group_counts, group_offsets):
    students, teachers = (
        lax.all_gather(student_hidden, ("wide", "narrow"), axis=0, tiled=True),
        lax.all_gather(teacher_hidden, ("wide", "narrow"), axis=0, tiled=True),
    )
    total = students.shape[0]
    groups = group_counts.shape[0]
    group_size = total // groups
    slots = jnp.arange(total, dtype=jnp.int32)
    group = slots // group_size
    within = slots % group_size
    match = group[:, None] == jnp.arange(groups, dtype=jnp.int32)[None, :]
    slot_counts = jnp.sum(jnp.where(match, group_counts[None, :], 0), axis=1)
    slot_offsets = jnp.sum(jnp.where(match, group_offsets[None, :], 0), axis=1)
    live = within < slot_counts
    pair = jnp.minimum(slot_offsets + within, total - 1)
    paired = jnp.take(teachers, pair, axis=0)
    student_logits = jnp.dot(students, student_head, preferred_element_type=jnp.float32)
    teacher_logits = jnp.dot(paired, teacher_head, preferred_element_type=jnp.float32)
    local_smax = jnp.max(student_logits, axis=1)
    local_tmax = jnp.max(teacher_logits, axis=1)
    smax, tmax = lax.pmax((local_smax, local_tmax), ("wide", "narrow"))
    sexp = jnp.exp(student_logits - smax[:, None])
    texp = jnp.exp(teacher_logits - tmax[:, None])
    ssum, tsum, tcross = lax.psum(
        (
            jnp.sum(sexp, axis=1),
            jnp.sum(texp, axis=1),
            jnp.sum(texp * (teacher_logits - student_logits), axis=1),
        ),
        ("wide", "narrow"),
    )
    value = tcross / tsum - tmax - jnp.log(tsum) + smax + jnp.log(ssum)
    kl_all = jnp.where(live, value, jnp.float32(0.0))
    diff = sexp / ssum[:, None] - texp / tsum[:, None]
    prob_diff = jnp.where(live[:, None], diff, jnp.float32(0.0)).astype(jnp.bfloat16)
    own_rows = student_hidden.shape[0]
    token_kl = lax.dynamic_slice_in_dim(
        kl_all, lax.axis_index(("wide", "narrow")) * own_rows, own_rows, 0
    )
    summed = lax.psum_scatter(
        lax.dot_general(
            prob_diff, student_head, (((1,), (1,)), ((), ())), preferred_element_type=jnp.float32
        ),
        ("wide", "narrow"),
        scatter_dimension=0,
        tiled=True,
    )
    return (token_kl, summed.astype(jnp.bfloat16))


def solution(mesh):
    return jax.shard_map(
        shards,
        mesh=mesh,
        in_specs=(
            P(("wide", "narrow"), None),
            P(("wide", "narrow"), None),
            P(None, ("wide", "narrow")),
            P(None, ("wide", "narrow")),
            P(),
            P(),
        ),
        out_specs=(P(("wide", "narrow")), P(("wide", "narrow"), None)),
        check_vma=False,
    )
```

profile of v0, /device:TPU:0, one launch (start us, length us, event | category | flops | bytes accessed | tf_op | source)
XLA Modules:
  0.0 437.4 jit_solution(2254615784137486701)
XLA Ops:
  7.2 0.0 all-gather.5.cloned.1.call-start
  7.2 0.7 all-gather.5.cloned.1.call-update
  7.9 0.0 all-gather.7.cloned.1.call-start
  7.9 0.7 all-gather.7.cloned.1.call-update
  8.7 0.8 select_reduce_fusion
  9.5 71.0 %all-gather.5.cloned.1.call-done = bf16[128,4,4096]{2,1,0:T(4,128)(2,1)} async-done(((bf16[1,4,4096]{2,1,0:T(4,128)(2,1)}), bf16[128,4,4096]{2,1,0:T(4,128)(2,1)}) %all-gather.5.cloned.1.call-update) | async-done | bytes 4194320 | tf_op jit(solution)/shard_map/all_gather | solution.py:10
  80.5 6.9 %reshape.84 = bf16[512,4096]{1,0:T(8,128)(2,1)} reshape(bf16[128,4,4096]{2,1,0:T(4,128)(2,1)} %all-gather.5.cloned.1.call-done) | data formatting | bytes 8388608
  87.4 11.3 %gather_fusion = bf16[512,4096]{1,0:T(8,128)(2,1)} fusion(bf16[512,4096]{1,0:T(8,128)(2,1)} %reshape.84, s32[1024]{0:T(1024)S(1)} %pad_clamp_fusion), kind=kCustom, calls=%fused_computation | custom fusion | bytes 8390656 | tf_op jit(solution)/shard_map/jit(_take)/gather | solution.py:23
  98.8 49.3 %all-gather.7.cloned.1.call-done = bf16[128,4,4096]{2,1,0:T(4,128)(2,1)} async-done(((bf16[1,4,4096]{2,1,0:T(4,128)(2,1)}), bf16[128,4,4096]{2,1,0:T(4,128)(2,1)}) %all-gather.7.cloned.1.call-update) | async-done | bytes 4194320 | tf_op jit(solution)/shard_map/all_gather | solution.py:9
  148.1 6.9 %reshape.86 = bf16[512,4096]{1,0:T(8,128)(2,1)} reshape(bf16[128,4,4096]{2,1,0:T(4,128)(2,1)} %all-gather.7.cloned.1.call-done) | data formatting | bytes 8388608
  155.0 0.0 copy-start
  155.0 10.4 %fusion.23 = (f32[512]{0:T(512)S(1)}, f32[512,1152]{1,0:T(8,128)S(1)}) fusion(bf16[512,4096]{1,0:T(8,128)(2,1)} %reshape.86, bf16[4096,1152]{1,0:T(8,128)(2,1)} %param.8), kind=kOutput, calls=%fused_computation.43 | convolution fusion | flops 4832427520 | bytes 15992832 | tf_op jit(solution)/shard_map/dot_general | solution.py:24
  165.4 0.0 copy-done
  165.4 9.9 %fusion.22 = (f32[512]{0:T(512)S(1)}, f32[512,1152]{1,0:T(8,128)}) fusion(bf16[4096,1152]{1,0:T(8,128)(2,1)} %param.9, bf16[512,4096]{1,0:T(8,128)(2,1)S(1)} %copy-done, pred[512]{0:T(512)(128)(4,1)S(1)} %compare_and_fusion), kind=kOutput, calls=%fused_computation.42 | convolution fusion | flops 4834524672 | bytes 15993344 | tf_op jit(solution)/shard_map/dot_general | solution.py:25
  175.3 62.8 %all-reduce.3 = (f32[512]{0:T(512)S(1)}, f32[512]{0:T(512)S(1)}) all-reduce(f32[512]{0:T(512)S(1)} %get-tuple-element.13, f32[512]{0:T(512)S(1)} %get-tuple-element.15), channel_id=1, replica_groups=mesh['wide'=32,'narrow'=4] {'wide','narrow'}, use_global_device_ids=true, to_apply=%region_3.4 | all-reduce | flops 1024 | bytes 8192 | tf_op jit(solution)/shard_map/pmax | solution.py:28
  238.1 2.7 multiply_reduce_fusion
  240.8 64.7 %all-reduce.2 = (f32[512]{0:T(512)S(1)}, f32[512]{0:T(512)S(1)}) all-reduce(f32[512]{0:T(512)S(1)} %get-tuple-element.4, f32[512]{0:T(512)S(1)} %get-tuple-element.3), channel_id=1, replica_groups=mesh['wide'=32,'narrow'=4] {'wide','narrow'}, use_global_device_ids=true, to_apply=%region_11.12 | all-reduce | flops 1024 | bytes 8192 | tf_op jit(solution)/shard_map/psum | solution.py:31
  305.5 12.5 %fusion.6 = f32[512,4096]{1,0:T(8,128)} fusion(bf16[4096,1152]{1,0:T(8,128)(2,1)} %param.8, f32[512,1152]{1,0:T(8,128)} %get-tuple-element.14, f32[512,1152]{1,0:T(8,128)S(1)} %get-tuple-element.16, f32[512]{0:T(512)S(1)} %get-tuple-element.10, f32[512]{0:T(512)S(1)} %get-tuple-element.9, f32[512]{0:T(512)S(1)} %get-tuple-element.12, ...), kind=kOutput, calls=%fused_computation.11 | convolution fusion | flops 4835966976 | bytes 22553088 | tf_op jit(solution)/shard_map/dot_general | solution.py:48
  318.0 110.5 %all-reduce.5 = (f32[512]{0:T(512)S(1)}, bf16[512,4096]{1,0:T(8,128)(2,1)}) all-reduce(f32[512]{0:T(512)S(1)} %get-tuple-element.2, f32[512,4096]{1,0:T(8,128)} %fusion.6), channel_id=1, replica_groups=mesh['wide'=32,'narrow'=4] {'wide','narrow'}, use_global_device_ids=true, to_apply=%region_5.6 | all-reduce | flops 2097664 | bytes 12587008 | tf_op jit(solution)/shard_map/psum | solution.py:31
  428.5 1.5 dynamic-slice_convert_fusion
  430.0 0.6 dynamic_slice.3
  (6 shorter events, 0.1 us)
Async XLA Ops:
  7.2 73.4 %all-gather.5.cloned.1.call-start = ((), (), s32[]{:S(2)}) async-start(), calls=%async_computation | async-start | bytes 4227072 | tf_op jit(solution)/shard_map/all_gather | solution.py:10
  7.9 140.2 %all-gather.7.cloned.1.call-start = ((), (), s32[]{:S(2)}) async-start(), calls=%async_computation.1 | async-start | bytes 4227072 | tf_op jit(solution)/shard_map/all_gather | solution.py:9
  155.0 10.4 %copy-start = (bf16[512,4096]{1,0:T(8,128)(2,1)S(1)}, bf16[512,4096]{1,0:T(8,128)(2,1)}, u32[]{:S(2)}) copy-start(bf16[512,4096]{1,0:T(8,128)(2,1)} %gather_fusion) | copy-start | bytes 12582916
Sparse Core Ops, SparseCore 0:
  11.1 69.3 all-gather.4
  83.7 64.3 all-gather.6
where the time goes:
time: 438 us; the launch traced here: 437 us
  blocking collectives  238 us (54%)
  waiting for transfers between devices  122 us (28%)
  matrix products  32.8 us (7%)
  local copies, waits for them, and re-layouts  27.2 us (6%)
  between operations  14.1 us (3%)
    psum x2, blocking collectives, shards(): lax.psum((jnp.sum(sexp, axis=1), jnp.sum(texp, axis=1), jnp.sum(texp * (t...  175 us
    all_gather x1, waiting for transfers between devices, shards(): lax.all_gather(teacher_hidden, ('wide', 'narrow'), axis=0, tiled=True)  71 us
    pmax x1, blocking collectives, shards(): smax, tmax = lax.pmax((local_smax, local_tmax), ('wide', 'narrow'))  62.8 us
    all_gather x1, waiting for transfers between devices, shards(): lax.all_gather(student_hidden, ('wide', 'narrow'), axis=0, tiled=True)  49.3 us
    unnamed x4, local copies, waits for them, and re-layouts  13.8 us
    dot_general x1, matrix products, shards(): lax.dot_general(prob_diff, student_head, (((1,), (1,)), ((), ())), prefer...  12.5 us
    gather x1, local copies, waits for them, and re-layouts, shards(): paired = jnp.take(teachers, pair, axis=0)  11.3 us
    dot_general x1, matrix products, shards(): jnp.dot(students, student_head, preferred_element_type=jnp.float32)  10.4 us
  transfers between devices with their start and end apart: 2, of which 2 were waited for; matrix products, arithmetic and copies ran while one was open for 4% of the time, Pallas kernels for 0%

commit v1 on v0

v1 whole, which is shorter than its diff:
```python
import jax
import jax.numpy as jnp
from jax import lax
from jax.experimental import pallas as pl
from jax.experimental.pallas import tpu as pltpu
from jax.sharding import PartitionSpec as P

MESH = pl.DeviceIdType.MESH
F32, BF16 = jnp.float32, jnp.bfloat16
AXES = ("z", "x", "y")
GATHER = ((0, 384, ("x", "y", "z")), (384, 384, ("y", "z", "x")), (768, 256, ("z", "x", "y")))
ORDERS = (("z", "x", "y"), ("x", "y", "z"), ("y", "z", "x"))
CHUNKS = 8
COPIES = 264
VOCAB = 1152
TILES = VOCAB // 128


def kernel(
    student_ref, teacher_ref, shead_hbm, thead_hbm, count_ref, offset_ref,
    kl_ref, grad_ref,
    shead, thead, xs, xt, sl, tl, et, pd,
    pre_send, pre_recv, block, stat, st_send, st_recv,
    core_send, core_recv, own, stage0, recv0, mid0, cur1, stage1, recv1, mid1, cur2, recv2, cur3, fin_send, fin_recv,
    send_sem, recv_sem, load_sem,
):
    wide = lax.axis_index("wide")
    me = {"z": lax.axis_index("narrow"), "x": wide // 8, "y": lax.rem(wide // 2, 4)}
    core = lax.rem(wide, 2)

    def device(at, c):
        return ((at["x"] * 4 + at["y"]) * 2 + c, at["z"])

    def shifted(axis, delta):
        return {**me, axis: lax.rem(me[axis] + delta, 4)}

    def peer(axis, delta):
        return device(shifted(axis, delta), core)

    sibling = device(me, 1 - core)
    started = []

    def send(src, dst, to):
        index = len(started)
        copy = pltpu.make_async_remote_copy(
            src_ref=src, dst_ref=dst, send_sem=send_sem.at[index], recv_sem=recv_sem.at[index],
            device_id=to, device_id_type=MESH,
        )
        copy.start()
        started.append(copy)
        return copy

    loads = [
        pltpu.make_async_copy(thead_hbm, thead, load_sem.at[0]),
        pltpu.make_async_copy(shead_hbm, shead, load_sem.at[1]),
    ]
    for load in loads:
        load.start()

    barrier = pltpu.get_barrier_semaphore()
    friends = [peer(axis, delta) for axis in AXES for delta in (1, 2, 3)] + [sibling]
    for friend in friends:
        pl.semaphore_signal(barrier, inc=1, device_id=friend, device_id_type=MESH)

    for q in range(4):
        pre_send[q, 0:4, :] = teacher_ref[:, q * 1024:(q + 1) * 1024].astype(F32)
        pre_send[q, 4:8, :] = student_ref[:, q * 1024:(q + 1) * 1024].astype(F32)
    pl.semaphore_wait(barrier, len(friends))

    z = me["z"]
    first = []
    for delta in (1, 2, 3):
        to = shifted("z", delta)
        first.append(send(pre_send.at[to["z"]], pre_recv.at[z], device(to, core)))
    pre_recv[z] = pre_send[z]
    for copy in first:
        copy.wait_recv()
    for row, rows in ((0, xt), (4, xs)):
        for s in range(4):
            block[4 * s:4 * s + 4, :] = pre_recv[s, row:row + 4, :]
        rows[z, me["x"], me["y"], core] = block[...].astype(BF16)

    def region(rows, part, free, at, c, half=None):
        start, width, order = GATHER[part]
        index = []
        for axis in AXES:
            if axis not in free:
                index.append(at[axis])
            elif half is not None and axis == order[0]:
                index.append(pl.ds(2 * half, 2))
            else:
                index.append(pl.ds(0, 4))
        return rows.at[(*index, c, pl.ds(0, 16), pl.ds(start, width))]

    parts = range(len(GATHER))

    def to_core(rows, part, free, at):
        here = region(rows, part, free, at, core)
        return send(here, here, sibling)

    def phase0(rows):
        copies = []
        for part in parts:
            axis = GATHER[part][2][0]
            here = region(rows, part, (), me, core)
            copies.append([send(here, here, peer(axis, delta)) for delta in (1, 3, 2)])
        return copies

    def start_phase(rows, step):
        copies = []
        for part in parts:
            order = GATHER[part][2]
            axis, free = order[step], order[:step]
            halves = [region(rows, part, free, me, core, half) for half in (0, 1)]
            group = {}
            group["l0"] = send(halves[0], halves[0], peer(axis, 1))
            group["r1"] = send(halves[1], halves[1], peer(axis, 3))
            group["l1"] = send(halves[1], halves[1], peer(axis, 1))
            group["r0"] = send(halves[0], halves[0], peer(axis, 3))
            copies.append(group)
        return copies

    def pass_on(rows, step, copies):
        for part in parts:
            order = GATHER[part][2]
            axis, free = order[step], order[:step]
            group = copies[part]
            group["l0"].wait_recv()
            here = region(rows, part, free, shifted(axis, 3), core, 0)
            group["lf"] = send(here, here, peer(axis, 1))
            group["r1"].wait_recv()
            here = region(rows, part, free, shifted(axis, 1), core, 1)
            group["rf"] = send(here, here, peer(axis, 3))

    def finish(copies, names):
        for group in copies:
            for name in names:
                group[name].wait_recv()

    def own_to_core(rows):
        return [to_core(rows, part, GATHER[part][2][:2], me) for part in parts]

    def near_to_core(rows, copies):
        finish(copies, ("l1", "r0"))
        return [
            to_core(rows, part, GATHER[part][2][:2], shifted(GATHER[part][2][2], delta))
            for part in parts for delta in (3, 1)
        ]

    def far_to_core(rows, copies):
        finish(copies, ("lf", "rf"))
        return [
            to_core(rows, part, GATHER[part][2][:2], shifted(GATHER[part][2][2], 2)) for part in parts
        ]

    t0 = phase0(xt)
    s0 = phase0(xs)
    for group in t0:
        for copy in group:
            copy.wait_recv()
    t1 = start_phase(xt, 1)
    for group in s0:
        for copy in group:
            copy.wait_recv()
    s1 = start_phase(xs, 1)
    pass_on(xt, 1, t1)
    pass_on(xs, 1, s1)
    finish(t1, ("l1", "r0", "lf", "rf"))
    t2 = start_phase(xt, 2)
    tcore = own_to_core(xt)
    finish(s1, ("l1", "r0", "lf", "rf"))
    pass_on(xt, 2, t2)
    s2 = start_phase(xs, 2)
    score = own_to_core(xs)
    tcore += near_to_core(xt, t2)
    tcore += far_to_core(xt, t2)
    for copy in tcore:
        copy.wait_recv()
    loads[0].wait()

    def logits(rows, head, out, tile, count):
        total = None
        for q in range(4):
            part = jnp.dot(
                rows[q].reshape(512, 1024),
                head[q * 1024:(q + 1) * 1024, tile * 128:(tile + count) * 128],
                preferred_element_type=F32,
            )
            total = part if total is None else total + part
        for i in range(count):
            out[tile + i] = total[:, i * 128:(i + 1) * 128]

    logits(xt, thead, tl, 0, 2)
    logits(xt, thead, tl, 2, 2)
    pass_on(xs, 2, s2)
    logits(xt, thead, tl, 4, 2)
    score += near_to_core(xs, s2)
    logits(xt, thead, tl, 6, 2)
    score += far_to_core(xs, s2)
    logits(xt, thead, tl, 8, 1)
    for copy in score:
        copy.wait_recv()
    loads[1].wait()
    for tile in (0, 2, 4, 6):
        logits(xs, shead, sl, tile, 2)
    logits(xs, shead, sl, 8, 1)

    lane = lax.broadcasted_iota(jnp.int32, (16, 128), 1)

    def terms(g, carry):
        at = pl.ds(pl.multiple_of(g * 16, 16), 16)
        pair = pl.ds(offset_ref[g], 16)
        s = [sl[j, at, :] for j in range(TILES)]
        t = [tl[j, pair, :] for j in range(TILES)]
        smax, tmax = s[0], t[0]
        for j in range(1, TILES):
            smax = jnp.maximum(smax, s[j])
            tmax = jnp.maximum(tmax, t[j])
        smax = jnp.max(smax, axis=1, keepdims=True)
        tmax = jnp.max(tmax, axis=1, keepdims=True)
        ssum = tsum = cross = jnp.zeros((16, 128), F32)
        for j in range(TILES):
            e = jnp.exp(s[j] - smax)
            sl[j, at, :] = e
            ssum = ssum + e
            e = jnp.exp(t[j] - tmax)
            et[j, at, :] = e
            tsum = tsum + e
            cross = cross + e * (t[j] - s[j])
        ssum = jnp.sum(ssum, axis=1, keepdims=True)
        tsum = jnp.sum(tsum, axis=1, keepdims=True)
        cross = jnp.sum(cross, axis=1, keepdims=True)
        tile = jnp.where(lane == 0, smax, jnp.where(lane == 1, tmax, jnp.where(lane == 2, ssum, jnp.where(lane == 3, tsum, cross))))
        stat[at, :] = tile
        return carry

    lax.fori_loop(0, 32, terms, 0, unroll=2)

    local = stat[...].T[0:8, :]
    now = local
    slot = 0
    for level, axis in enumerate(("core", "x", "y", "z")):
        st_send[level] = now
        if axis == "core":
            copies = [send(st_send.at[level], st_recv.at[slot], sibling)]
        else:
            copies = [
                send(st_send.at[level], st_recv.at[slot + i], peer(axis, delta))
                for i, delta in enumerate((1, 3, 2))
            ]
        for copy in copies:
            copy.wait_recv()
        members = [now] + [st_recv[slot + i] for i in range(len(copies))]
        slot += len(copies)
        smax, tmax = members[0][0:1], members[0][1:2]
        for member in members[1:]:
            smax = jnp.maximum(smax, member[0:1])
            tmax = jnp.maximum(tmax, member[1:2])
        ssum = tsum = cross = jnp.zeros((1, 512), F32)
        for member in members:
            a = jnp.exp(member[0:1] - smax)
            b = jnp.exp(member[1:2] - tmax)
            ssum = ssum + member[2:3] * a
            tsum = tsum + member[3:4] * b
            cross = cross + member[4:5] * b
        now = jnp.concatenate([smax, tmax, ssum, tsum, cross, cross, cross, cross], axis=0)
    value = cross / tsum - tmax - jnp.log(tsum) + smax + jnp.log(ssum)
    sscale = jnp.exp(local[0:1] - smax) / ssum
    tscale = jnp.exp(local[1:2] - tmax) / tsum
    filler = jnp.zeros((125, 512), F32)
    stat[...] = jnp.concatenate([sscale, tscale, value, filler], axis=0).T

    row = lax.broadcasted_iota(jnp.int32, (16, 128), 0)
    mine = stat[pl.ds(pl.multiple_of(wide * 16, 16), 16), :]
    mine = jnp.where(row < count_ref[wide], mine, 0.0)
    for i in range(4):
        kl_ref[i] = jnp.sum(jnp.where((row == z * 4 + i) & (lane == 2), mine, 0.0))

    def prob_diff(pair, carry):
        for c in range(2):
            g = pair * 2 + c
            half = core if c else 1 - core
            at = pl.ds(pl.multiple_of(g * 16, 16), 16)
            scale = stat[at, :]
            live = row < count_ref[g]
            a = jnp.where(live, jnp.broadcast_to(scale[:, 0:1], (16, 128)), 0.0)
            b = jnp.where(live, jnp.broadcast_to(scale[:, 1:2], (16, 128)), 0.0)
            for j in range(TILES):
                pd[half, pair, :, j * 128:(j + 1) * 128] = (sl[j, at, :] * a - et[j, at, :] * b).astype(BF16)
        return carry

    lax.fori_loop(0, 16, prob_diff, 0)

    def grad_matmul(j):
        weights = jnp.concatenate([shead[q * 1024 + j * 128:q * 1024 + (j + 1) * 128, :] for q in range(4)], axis=0)
        out = lax.dot_general(
            pd[...].reshape(512, VOCAB), weights, (((1,), (1,)), ((), ())), preferred_element_type=F32
        )
        for q in range(4):
            piece = out[:, q * 128:(q + 1) * 128]
            core_send[j, q] = piece[0:256].astype(BF16).reshape(4, 4, 16, 128)
            own[j, q] = piece[256:512].reshape(4, 4, 16, 128)
        return send(core_send.at[j], core_recv.at[j], sibling)

    def pick(ref, j, axis, axes, q):
        index = [slice(None)] * len(axes)
        index[axes.index(axis)] = q
        return ref[(j, *index)]

    def scatter_start(j, cur, axis, axes, stage, recv, mid):
        right, left = peer(axis, 1), peer(axis, 3)
        stage[j, 2] = pick(cur, j, axis, axes, lax.rem(me[axis] + 2, 4)).astype(BF16)
        copies = {}
        copies["lm"] = send(stage.at[j, 2, pl.ds(0, 2)], mid.at[j, 0], right)
        copies["rm"] = send(stage.at[j, 2, pl.ds(2, 2)], mid.at[j, 1], left)
        stage[j, 0, 2:4] = pick(cur, j, axis, axes, lax.rem(me[axis] + 1, 4))[2:4].astype(BF16)
        stage[j, 1, 0:2] = pick(cur, j, axis, axes, lax.rem(me[axis] + 3, 4))[0:2].astype(BF16)
        copies["l1"] = send(stage.at[j, 0, pl.ds(2, 2)], recv.at[j, 0, pl.ds(2, 2)], right)
        copies["r0"] = send(stage.at[j, 1, pl.ds(0, 2)], recv.at[j, 1, pl.ds(0, 2)], left)
        return copies

    def scatter_pass(j, cur, axis, axes, stage, recv, mid, copies):
        right, left = peer(axis, 1), peer(axis, 3)
        copies["lm"].wait_recv()
        ours = pick(cur, j, axis, axes, lax.rem(me[axis] + 1, 4))[0:2]
        stage[j, 0, 0:2] = (ours + mid[j, 0].astype(F32)).astype(BF16)
        copies["l0"] = send(stage.at[j, 0, pl.ds(0, 2)], recv.at[j, 0, pl.ds(0, 2)], right)
        copies["rm"].wait_recv()
        ours = pick(cur, j, axis, axes, lax.rem(me[axis] + 3, 4))[2:4]
        stage[j, 1, 2:4] = (ours + mid[j, 1].astype(F32)).astype(BF16)
        copies["r1"] = send(stage.at[j, 1, pl.ds(2, 2)], recv.at[j, 1, pl.ds(2, 2)], left)

    def scatter_end(j, cur, axis, axes, recv, copies):
        for name in ("l1", "r0", "l0", "r1"):
            copies[name].wait_recv()
        return pick(cur, j, axis, axes, me[axis]) + recv[j, 0].astype(F32) + recv[j, 1].astype(F32)

    state = [{} for _ in range(CHUNKS)]

    def axes_of(j):
        order = ORDERS[j % 3]
        after = tuple(axis for axis in AXES if axis != order[0])
        return order, after

    def step(j, level):
        order, after = axes_of(j)
        mem = state[j]
        if level == 0:
            mem["core"] = grad_matmul(j)
        elif level == 1:
            mem["core"].wait_recv()
            own[j] = own[j] + core_recv[j].astype(F32)
            mem["a"] = scatter_start(j, own, order[0], AXES, stage0, recv0, mid0)
        elif level == 2:
            scatter_pass(j, own, order[0], AXES, stage0, recv0, mid0, mem["a"])
        elif level == 3:
            cur1[j] = scatter_end(j, own, order[0], AXES, recv0, mem["a"])
            mem["b"] = scatter_start(j, cur1, order[1], after, stage1, recv1, mid1)
        elif level == 4:
            scatter_pass(j, cur1, order[1], after, stage1, recv1, mid1, mem["b"])
        elif level == 5:
            cur2[j] = scatter_end(j, cur1, order[1], after, recv1, mem["b"])
            mem["c"] = [
                send(cur2.at[j, shifted(order[2], delta)[order[2]]], recv2.at[j, i], peer(order[2], delta))
                for i, delta in enumerate((1, 3, 2))
            ]
        else:
            for copy in mem["c"]:
                copy.wait_recv()
            cur3[:, j * 128:(j + 1) * 128] = cur2[j, me[order[2]]] + recv2[j, 0] + recv2[j, 1] + recv2[j, 2]

    for time in range(CHUNKS + 6):
        for level in range(6, -1, -1):
            if 0 <= time - level < CHUNKS:
                step(time - level, level)

    for q in range(4):
        fin_send[q] = cur3[4 * q:4 * q + 4, :]
    last = []
    for delta in (1, 2, 3):
        to = shifted("z", delta)
        last.append(send(fin_send.at[to["z"]], fin_recv.at[z], device(to, core)))
    fin_recv[z] = fin_send[z]
    for copy in last:
        copy.wait_recv()
    for q in range(4):
        grad_ref[:, q * 1024:(q + 1) * 1024] = fin_recv[q].astype(BF16)
    for copy in started:
        copy.wait_send()


def shards(student_hidden, teacher_hidden, student_head, teacher_head, group_counts, group_offsets):
    vmem = pl.BlockSpec(memory_space=pltpu.VMEM)
    smem = pl.BlockSpec(memory_space=pltpu.SMEM)
    hbm = pl.BlockSpec(memory_space=pl.ANY)
    rows = pltpu.VMEM((4, 4, 4, 2, 16, 1024), BF16)
    head = pltpu.VMEM((4096, VOCAB), BF16)
    table = pltpu.VMEM((TILES, 512, 128), F32)
    scratch = [
        head, head, rows, rows, table, table, table,
        pltpu.VMEM((2, 16, 16, VOCAB), BF16),
        pltpu.VMEM((4, 8, 1024), F32),
        pltpu.VMEM((4, 8, 1024), F32),
        pltpu.VMEM((16, 1024), F32),
        pltpu.VMEM((512, 128), F32),
        pltpu.VMEM((4, 8, 512), F32),
        pltpu.VMEM((10, 8, 512), F32),
        pltpu.VMEM((CHUNKS, 4, 4, 4, 16, 128), BF16),
        pltpu.VMEM((CHUNKS, 4, 4, 4, 16, 128), BF16),
        pltpu.VMEM((CHUNKS, 4, 4, 4, 16, 128), F32),
        pltpu.VMEM((CHUNKS, 3, 4, 4, 16, 128), BF16),
        pltpu.VMEM((CHUNKS, 2, 4, 4, 16, 128), BF16),
        pltpu.VMEM((CHUNKS, 2, 2, 4, 16, 128), BF16),
        pltpu.VMEM((CHUNKS, 4, 4, 16, 128), F32),
        pltpu.VMEM((CHUNKS, 3, 4, 16, 128), BF16),
        pltpu.VMEM((CHUNKS, 2, 4, 16, 128), BF16),
        pltpu.VMEM((CHUNKS, 2, 2, 16, 128), BF16),
        pltpu.VMEM((CHUNKS, 4, 16, 128), F32),
        pltpu.VMEM((CHUNKS, 3, 16, 128), F32),
        pltpu.VMEM((16, 1024), F32),
        pltpu.VMEM((4, 4, 1024), F32),
        pltpu.VMEM((4, 4, 1024), F32),
        pltpu.SemaphoreType.DMA((COPIES,)),
        pltpu.SemaphoreType.DMA((COPIES,)),
        pltpu.SemaphoreType.DMA((2,)),
    ]
    return pl.pallas_call(
        kernel,
        out_shape=(
            jax.ShapeDtypeStruct((4,), F32),
            jax.ShapeDtypeStruct((4, 4096), BF16),
        ),
        in_specs=[vmem, vmem, hbm, hbm, smem, smem],
        out_specs=(smem, vmem),
        scratch_shapes=scratch,
        compiler_params=pltpu.CompilerParams(
            collective_id=0, has_side_effects=True, vmem_limit_bytes=60 << 20
        ),
        cost_estimate=pl.CostEstimate(flops=14495514624, bytes_accessed=19000000, transcendentals=1200000),
    )(student_hidden, teacher_hidden, student_head, teacher_head, group_counts, group_offsets)


def solution(mesh):
    both = ("wide", "narrow")
    return jax.shard_map(
        shards,
        mesh=mesh,
        in_specs=(P(both, None), P(both, None), P(None, both), P(None, both), P(), P()),
        out_specs=(P(both), P(both, None)),
        check_vma=False,
    )
```

time: 438 us -> 124 us (0.28)
  blocking collectives: 238 us -> 0 us
  waiting for transfers between devices: 122 us -> 0 us
  Pallas kernels: 0 us -> 120 us
  matrix products: 32.8 us -> 0 us
  local copies, waits for them, and re-layouts: 27.2 us -> 2.56 us
  between operations: 14.1 us -> 0.64 us
    psum x2 -> x0, blocking collectives: 175 us -> none  [shards(): lax.psum((jnp.sum(sexp, axis=1), jnp.sum(texp, axis=1), jnp.sum(texp * (t...]
    all_gather x2 -> x0, waiting for transfers between devices: 120 us -> none  [the longest x1 71 us: shards(): lax.all_gather(teacher_hidden, ('wide', 'narrow'), axis=0, tiled=True)]
    pallas_call x0 -> x1, Pallas kernels: none -> 120 us  [shards(): pl.pallas_call(kernel, out_shape=(jax.ShapeDtypeStruct((4,), F32), jax.Sh...]
    pmax x1 -> x0, blocking collectives: 62.8 us -> none  [shards(): smax, tmax = lax.pmax((local_smax, local_tmax), ('wide', 'narrow'))]
    dot_general x3 -> x0, matrix products: 32.8 us -> none  [the longest x1 12.5 us: shards(): lax.dot_general(prob_diff, student_head, (((1,), (1,)), ((), ())), prefer...]
    gather x1 -> x0, local copies, waits for them, and re-layouts: 11.3 us -> none  [shards(): paired = jnp.take(teachers, pair, axis=0)]
    unnamed x4 -> x2, local copies, waits for them, and re-layouts: 13.8 us -> 2.56 us
  transfers between devices with their start and end apart: 2 -> 0, of which waited for: 2 -> 0; matrix products, arithmetic and copies ran while one was open for 4% -> 0% of each run, Pallas kernels for 0% -> 0%
where the time goes in v1:
time: 124 us; the launch traced here: 123 us
  Pallas kernels  120 us (97%)
  local copies, waits for them, and re-layouts  2.56 us (2%)
    pallas_call x1, Pallas kernels, shards(): pl.pallas_call(kernel, out_shape=(jax.ShapeDtypeStruct((4,), F32), jax.Sh...  120 us
    unnamed x2, local copies, waits for them, and re-layouts  2.56 us

profile of v1, /device:TPU:0, one launch (start us, length us, event | category | flops | bytes accessed | tf_op | source)
XLA Modules:
  0.0 123.4 jit_solution(15977466669423328336)
XLA Ops:
  0.6 120.2 %shard_map.77 = (f32[4]{0:T(128)}, bf16[4,4096]{1,0:T(4,128)(2,1)}) custom-call(bf16[4,4096]{1,0:T(4,128)(2,1)} %student_ref.1, bf16[4,4096]{1,0:T(4,128)(2,1)} %teacher_ref.1, bf16[4096,1152]{1,0:T(8,128)(2,1)} %shead_hbm.1, bf16[4096,1152]{1,0:T(8,128)(2,1)} %thead_hbm.1, s32[32]{0:T(128)} %count_ref.1, s32[32]{0:T(128)} %offset_ref.1), custom_call_target="tpu_custom_call" | custom-call | flops 14495514624 | bytes 19000000 | tf_op jit(solution)/shard_map/pallas_call | solution.py:427
  120.8 1.2 copy.10
  122.0 1.4 %copy.11 = bf16[4,4096]{1,0:T(4,128)(2,1)} copy(bf16[4,4096]{1,0:T(4,128)(2,1)} %get-tuple-element.5) | data formatting | bytes 65536

commit v2 on v1

v2 whole, which is shorter than its diff:
```python
import jax
import jax.numpy as jnp
from jax import lax
from jax.experimental import pallas as pl
from jax.experimental.pallas import tpu as pltpu
from jax.sharding import PartitionSpec as P

MESH = pl.DeviceIdType.MESH
F32, BF16 = jnp.float32, jnp.bfloat16
AXES = ("z", "x", "y")
GATHER = ((0, 384, ("x", "y", "z")), (384, 384, ("y", "z", "x")), (768, 256, ("z", "x", "y")))
FIRST = ("z", "z", "x", "x", "x", "y", "y", "y")
THEN = {"z": "x", "x": "y", "y": "x"}
SEQUENCE = (0, 2, 5, 1, 3, 6, 4, 7)
CHUNKS = len(FIRST)
COPIES = 208
FAR_FIRST = (2, 1, 3)
VOCAB = 1152
TILES = VOCAB // 128


def kernel(
    student_hbm, teacher_hbm, shead_hbm, thead_hbm, count_hbm, offset_hbm,
    out_ref,
    student_ref, teacher_ref, count_ref, offset_ref,
    shead, thead, rows, sl, tl, et, pd,
    pre_send, pre_recv, block, stat, st_send, st_recv,
    core_send, core_recv, own, stage0, recv0,
    curz, curx, cury, stagez, stagex, stagey, recvz, recvx, recvy, curz2, recvz2,
    finz, finx, finy, gotz, gotx, goty,
    send_sem, recv_sem, load_sem,
):
    wide = lax.axis_index("wide")
    me = {"z": lax.axis_index("narrow"), "x": wide // 8, "y": lax.rem(wide // 2, 4)}
    core = lax.rem(wide, 2)

    def device(at, c):
        return ((at["x"] * 4 + at["y"]) * 2 + c, at["z"])

    def shifted(axis, delta):
        return {**me, axis: lax.rem(me[axis] + delta, 4)}

    def peer(axis, delta):
        return device(shifted(axis, delta), core)

    sibling = device(me, 1 - core)
    started = []

    def send(src, dst, to):
        index = len(started)
        copy = pltpu.make_async_remote_copy(
            src_ref=src, dst_ref=dst, send_sem=send_sem.at[index], recv_sem=recv_sem.at[index],
            device_id=to, device_id_type=MESH,
        )
        copy.start()
        started.append(copy)
        return copy

    loads = [
        pltpu.make_async_copy(src, dst, load_sem.at[i])
        for i, (src, dst) in enumerate((
            (teacher_hbm, teacher_ref), (student_hbm, student_ref), (count_hbm, count_ref),
            (offset_hbm, offset_ref), (thead_hbm, thead), (shead_hbm, shead),
        ))
    ]
    for load in loads:
        load.start()

    barrier = pltpu.get_barrier_semaphore()
    friends = [peer(axis, delta) for axis in AXES for delta in (1, 2, 3)] + [sibling]
    for friend in friends:
        pl.semaphore_signal(barrier, inc=1, device_id=friend, device_id_type=MESH)

    for load in loads[:2]:
        load.wait()
    for q in range(4):
        pre_send[q, 0:4, :] = teacher_ref[:, q * 1024:(q + 1) * 1024].astype(F32)
        pre_send[q, 4:8, :] = student_ref[:, q * 1024:(q + 1) * 1024].astype(F32)
    pl.semaphore_wait(barrier, len(friends))

    z = me["z"]
    first = []
    for delta in (1, 2, 3):
        to = shifted("z", delta)
        first.append(send(pre_send.at[to["z"]], pre_recv.at[z], device(to, core)))
    pre_recv[z] = pre_send[z]
    for copy in first:
        copy.wait_recv()
    for which in range(2):
        for s in range(4):
            block[4 * s:4 * s + 4, :] = pre_recv[s, 4 * which:4 * which + 4, :]
        rows[which, z, me["x"], me["y"], core] = block[...].astype(BF16)

    def region(part, free, at, c, which=None, half=None):
        start, width, order = GATHER[part]
        index = [pl.ds(0, 2) if which is None else which]
        for axis in AXES:
            if axis not in free:
                index.append(at[axis])
            elif half is not None and axis == order[0]:
                index.append(pl.ds(2 * half, 2))
            else:
                index.append(pl.ds(0, 4))
        return rows.at[(*index, c, pl.ds(0, 16), pl.ds(start, width))]

    parts = range(len(GATHER))

    def spread(part, step):
        order = GATHER[part][2]
        here = region(part, order[:step], me, core)
        return [send(here, here, peer(order[step], delta)) for delta in FAR_FIRST]

    def to_core(part, at, which=None):
        here = region(part, GATHER[part][2][:2], at, core, which)
        return send(here, here, sibling)

    def start_last(which, names):
        for part in parts:
            order = GATHER[part][2]
            for name in names:
                here = region(part, order[:2], me, core, which, int(name[1]))
                last[which][part][name] = send(here, here, peer(order[2], 1 if name[0] == "l" else 3))

    def pass_on(which):
        for part in parts:
            order = GATHER[part][2]
            for name, delta, half, to in (("l0", 3, 0, 1), ("r1", 1, 1, 3)):
                last[which][part][name].wait_recv()
                here = region(part, order[:2], shifted(order[2], delta), core, which, half)
                last[which][part]["far" + name] = send(here, here, peer(order[2], to))

    def near_to_core(which):
        copies = []
        for part in parts:
            for name, delta in (("l1", 3), ("r0", 1)):
                last[which][part][name].wait_recv()
                copies.append(to_core(part, shifted(GATHER[part][2][2], delta), which))
        return copies

    def far_to_core(which):
        copies = []
        for part in parts:
            for name in ("farl0", "farr1"):
                last[which][part][name].wait_recv()
            copies.append(to_core(part, shifted(GATHER[part][2][2], 2), which))
        return copies

    last = [[{} for _ in parts] for _ in range(2)]
    step0 = [spread(part, 0) for part in parts]
    step1 = []
    for part in parts:
        for copy in step0[part]:
            copy.wait_recv()
        step1.append(spread(part, 1))
    for part in parts:
        for copy in step1[part]:
            copy.wait_recv()
    start_last(0, ("l0", "r1", "l1", "r0"))
    start_last(1, ("l0", "r1"))
    cores = [[to_core(part, me) for part in parts], []]
    pass_on(0)
    start_last(1, ("l1", "r0"))
    cores[0] += near_to_core(0)
    cores[0] += far_to_core(0)
    for copy in cores[0]:
        copy.wait_recv()
    loads[4].wait()

    def logits(which, head, out, tile):
        count = min(2, TILES - tile)
        total = None
        for q in range(4):
            part = jnp.dot(
                rows[which, q].reshape(512, 1024),
                head[q * 1024:(q + 1) * 1024, tile * 128:(tile + count) * 128],
                preferred_element_type=F32,
            )
            total = part if total is None else total + part
        for i in range(count):
            out[tile + i] = total[:, i * 128:(i + 1) * 128]

    logits(0, thead, tl, 0)
    pass_on(1)
    logits(0, thead, tl, 2)
    logits(0, thead, tl, 4)
    cores[1] += near_to_core(1)
    logits(0, thead, tl, 6)
    cores[1] += far_to_core(1)
    logits(0, thead, tl, 8)
    for copy in cores[1]:
        copy.wait_recv()
    for load in (loads[2], loads[3], loads[5]):
        load.wait()
    for tile in range(0, TILES, 2):
        logits(1, shead, sl, tile)

    lane = lax.broadcasted_iota(jnp.int32, (16, 128), 1)

    def terms(g, carry):
        at = pl.ds(pl.multiple_of(g * 16, 16), 16)
        pair = pl.ds(offset_ref[g], 16)
        s = [sl[j, at, :] for j in range(TILES)]
        t = [tl[j, pair, :] for j in range(TILES)]
        smax, tmax = s[0], t[0]
        for j in range(1, TILES):
            smax = jnp.maximum(smax, s[j])
            tmax = jnp.maximum(tmax, t[j])
        smax = jnp.max(smax, axis=1, keepdims=True)
        tmax = jnp.max(tmax, axis=1, keepdims=True)
        ssum = tsum = cross = jnp.zeros((16, 128), F32)
        for j in range(TILES):
            e = jnp.exp(s[j] - smax)
            sl[j, at, :] = e
            ssum = ssum + e
            e = jnp.exp(t[j] - tmax)
            et[j, at, :] = e
            tsum = tsum + e
            cross = cross + e * (t[j] - s[j])
        ssum = jnp.sum(ssum, axis=1, keepdims=True)
        tsum = jnp.sum(tsum, axis=1, keepdims=True)
        cross = jnp.sum(cross, axis=1, keepdims=True)
        tile = jnp.where(lane == 0, smax, jnp.where(lane == 1, tmax, jnp.where(lane == 2, ssum, jnp.where(lane == 3, tsum, cross))))
        stat[at, :] = tile
        return carry

    lax.fori_loop(0, 32, terms, 0, unroll=4)

    local = stat[...].T[0:8, :]
    now = local
    slot = 0
    for level, axis in enumerate(("core", "x", "y", "z")):
        st_send[level] = now
        if axis == "core":
            copies = [send(st_send.at[level], st_recv.at[slot], sibling)]
        else:
            copies = [
                send(st_send.at[level], st_recv.at[slot + i], peer(axis, delta))
                for i, delta in enumerate(FAR_FIRST)
            ]
        for copy in copies:
            copy.wait_recv()
        members = [now] + [st_recv[slot + i] for i in range(len(copies))]
        slot += len(copies)
        smax, tmax = members[0][0:1], members[0][1:2]
        for member in members[1:]:
            smax = jnp.maximum(smax, member[0:1])
            tmax = jnp.maximum(tmax, member[1:2])
        ssum = tsum = cross = jnp.zeros((1, 512), F32)
        for member in members:
            a = jnp.exp(member[0:1] - smax)
            b = jnp.exp(member[1:2] - tmax)
            ssum = ssum + member[2:3] * a
            tsum = tsum + member[3:4] * b
            cross = cross + member[4:5] * b
        now = jnp.concatenate([smax, tmax, ssum, tsum, cross, cross, cross, cross], axis=0)
    value = cross / tsum - tmax - jnp.log(tsum) + smax + jnp.log(ssum)
    sscale = jnp.exp(local[0:1] - smax) / ssum
    tscale = jnp.exp(local[1:2] - tmax) / tsum
    filler = jnp.zeros((125, 512), F32)
    stat[...] = jnp.concatenate([sscale, tscale, value, filler], axis=0).T

    row = lax.broadcasted_iota(jnp.int32, (16, 128), 0)
    four = lax.broadcasted_iota(jnp.int32, (4, 128), 0)
    mine = stat[pl.ds(wide * 16 + z * 4, 4), :]
    mine = jnp.where(four + z * 4 < count_ref[wide], jnp.broadcast_to(mine[:, 2:3], (4, 128)), 0.0)
    out_ref[:, 4096:4224] = mine

    def prob_diff(pair, carry):
        for c in range(2):
            g = pair * 2 + c
            half = core if c else 1 - core
            at = pl.ds(pl.multiple_of(g * 16, 16), 16)
            scale = stat[at, :]
            live = row < count_ref[g]
            a = jnp.where(live, jnp.broadcast_to(scale[:, 0:1], (16, 128)), 0.0)
            b = jnp.where(live, jnp.broadcast_to(scale[:, 1:2], (16, 128)), 0.0)
            for j in range(TILES):
                pd[half, pair, :, j * 128:(j + 1) * 128] = (sl[j, at, :] * a - et[j, at, :] * b).astype(BF16)
        return carry

    lax.fori_loop(0, 16, prob_diff, 0)

    def grad_matmul(j):
        weights = jnp.concatenate([shead[q * 1024 + j * 128:q * 1024 + (j + 1) * 128, :] for q in range(4)], axis=0)
        out = lax.dot_general(
            pd[...].reshape(512, VOCAB), weights, (((1,), (1,)), ((), ())), preferred_element_type=F32
        )
        for q in range(4):
            piece = out[:, q * 128:(q + 1) * 128]
            core_send[j, q] = piece[0:256].astype(BF16).reshape(4, 4, 16, 128)
            own[j, q] = piece[256:512].reshape(4, 4, 16, 128)
        return send(core_send.at[j], core_recv.at[j], sibling)

    def pick(ref, j, axis, q):
        index = [slice(None)] * 3
        index[AXES.index(axis)] = q
        return ref[(j, *index)]

    boxes = {}

    def first_start(j, core_copy):
        axis = FIRST[j]
        core_copy.wait_recv()
        boxes[j] = []
        for i, delta in enumerate(FAR_FIRST):
            q = shifted(axis, delta)[axis]
            stage0[j, i] = (pick(own, j, axis, q) + pick(core_recv, j, axis, q).astype(F32)).astype(BF16)
            boxes[j].append(send(stage0.at[j, i], recv0.at[j, i], peer(axis, delta)))

    cur = {"z": curz, "x": curx, "y": cury}
    stage = {"z": stagez, "x": stagex, "y": stagey}
    recv = {"z": recvz, "x": recvx, "y": recvy}

    def first_end(j):
        axis = FIRST[j]
        for copy in boxes[j]:
            copy.wait_recv()
        total = pick(own, j, axis, me[axis]) + pick(core_recv, j, axis, me[axis]).astype(F32)
        for i in range(3):
            total = total + recv0[j, i].astype(F32)
        place = j - FIRST.index(axis)
        for q in range(4):
            cur[axis][q, place] = total[q] if axis == "z" else total[:, q]

    def second_start(axis):
        copies = []
        for i, delta in enumerate(FAR_FIRST):
            q = shifted(THEN[axis], delta)[THEN[axis]]
            stage[axis][i] = cur[axis][q].astype(BF16)
            copies.append(send(stage[axis].at[i], recv[axis].at[i], peer(THEN[axis], delta)))
        return copies

    def second_end(axis, copies):
        for copy in copies:
            copy.wait_recv()
        total = cur[axis][me[THEN[axis]]]
        for i in range(3):
            total = total + recv[axis][i].astype(F32)
        return total

    def rows_start(total, fin, got):
        for q in range(4):
            fin[q] = total[:, :, 4 * q:4 * q + 4, :]
        copies = []
        for delta in FAR_FIRST:
            q = shifted("z", delta)["z"]
            copies.append(send(fin.at[q], got.at[z], peer("z", delta)))
        got[z] = fin[z]
        return copies

    waiting = []
    for n, j in enumerate(SEQUENCE):
        waiting.append((j, grad_matmul(j)))
        if n >= 1:
            first_start(*waiting.pop(0))
    first_start(*waiting.pop(0))

    for j in (0, 1):
        first_end(j)
    zcopies = second_start("z")
    for j in (2, 3, 4):
        first_end(j)
    xcopies = second_start("x")
    for j in (5, 6, 7):
        first_end(j)
    ycopies = second_start("y")
    total = second_end("z", zcopies)
    for q in range(4):
        curz2[q] = total[:, q]
    zcopies = [
        send(curz2.at[shifted("y", delta)["y"]], recvz2.at[i], peer("y", delta))
        for i, delta in enumerate(FAR_FIRST)
    ]
    xcopies = rows_start(second_end("x", xcopies), finx, gotx)
    ycopies = rows_start(second_end("y", ycopies), finy, goty)
    for copy in zcopies:
        copy.wait_recv()
    total = curz2[me["y"]] + recvz2[0] + recvz2[1] + recvz2[2]
    zcopies = rows_start(total[None], finz, gotz)
    for axis, copies, got in (("x", xcopies, gotx), ("y", ycopies, goty)):
        for copy in copies:
            copy.wait_recv()
        total = got[0] + got[1] + got[2] + got[3]
        for place in range(3):
            for q in range(4):
                at = q * 1024 + (FIRST.index(axis) + place) * 128
                out_ref[:, at:at + 128] = total[place, q]
    for copy in zcopies:
        copy.wait_recv()
    for place in range(2):
        for q in range(4):
            at = q * 1024 + place * 128
            out_ref[:, at:at + 128] = gotz[q, 0, place]
    for copy in started:
        copy.wait_send()


def shards(student_hidden, teacher_hidden, student_head, teacher_head, group_counts, group_offsets):
    hbm = pl.BlockSpec(memory_space=pl.ANY)
    head = pltpu.VMEM((4096, VOCAB), BF16)
    table = pltpu.VMEM((TILES, 512, 128), F32)
    scratch = [
        pltpu.VMEM((4, 4096), BF16),
        pltpu.VMEM((4, 4096), BF16),
        pltpu.SMEM((32,), jnp.int32),
        pltpu.SMEM((32,), jnp.int32),
        head, head,
        pltpu.VMEM((2, 4, 4, 4, 2, 16, 1024), BF16),
        table, table, table,
        pltpu.VMEM((2, 16, 16, VOCAB), BF16),
        pltpu.VMEM((4, 8, 1024), F32),
        pltpu.VMEM((4, 8, 1024), F32),
        pltpu.VMEM((16, 1024), F32),
        pltpu.VMEM((512, 128), F32),
        pltpu.VMEM((4, 8, 512), F32),
        pltpu.VMEM((10, 8, 512), F32),
        pltpu.VMEM((CHUNKS, 4, 4, 4, 16, 128), BF16),
        pltpu.VMEM((CHUNKS, 4, 4, 4, 16, 128), BF16),
        pltpu.VMEM((CHUNKS, 4, 4, 4, 16, 128), F32),
        pltpu.VMEM((CHUNKS, 3, 4, 4, 16, 128), BF16),
        pltpu.VMEM((CHUNKS, 3, 4, 4, 16, 128), BF16),
        pltpu.VMEM((4, 2, 4, 16, 128), F32),
        pltpu.VMEM((4, 3, 4, 16, 128), F32),
        pltpu.VMEM((4, 3, 4, 16, 128), F32),
        pltpu.VMEM((3, 2, 4, 16, 128), BF16),
        pltpu.VMEM((3, 3, 4, 16, 128), BF16),
        pltpu.VMEM((3, 3, 4, 16, 128), BF16),
        pltpu.VMEM((3, 2, 4, 16, 128), BF16),
        pltpu.VMEM((3, 3, 4, 16, 128), BF16),
        pltpu.VMEM((3, 3, 4, 16, 128), BF16),
        pltpu.VMEM((4, 2, 16, 128), F32),
        pltpu.VMEM((3, 2, 16, 128), F32),
        pltpu.VMEM((4, 1, 2, 4, 128), F32),
        pltpu.VMEM((4, 3, 4, 4, 128), F32),
        pltpu.VMEM((4, 3, 4, 4, 128), F32),
        pltpu.VMEM((4, 1, 2, 4, 128), F32),
        pltpu.VMEM((4, 3, 4, 4, 128), F32),
        pltpu.VMEM((4, 3, 4, 4, 128), F32),
        pltpu.SemaphoreType.DMA((COPIES,)),
        pltpu.SemaphoreType.DMA((COPIES,)),
        pltpu.SemaphoreType.DMA((6,)),
    ]
    out = pl.pallas_call(
        kernel,
        out_shape=jax.ShapeDtypeStruct((4, 4224), F32),
        in_specs=[hbm] * 6,
        out_specs=pl.BlockSpec(memory_space=pltpu.VMEM),
        scratch_shapes=scratch,
        compiler_params=pltpu.CompilerParams(
            collective_id=0, has_side_effects=True, vmem_limit_bytes=60 << 20
        ),
        cost_estimate=pl.CostEstimate(flops=14495514624, bytes_accessed=19000000, transcendentals=1200000),
    )(student_hidden, teacher_hidden, student_head, teacher_head, group_counts, group_offsets)
    return out[:, 4096], out[:, :4096].astype(BF16)


def solution(mesh):
    both = ("wide", "narrow")
    return jax.shard_map(
        shards,
        mesh=mesh,
        in_specs=(P(both, None), P(both, None), P(None, both), P(None, both), P(), P()),
        out_specs=(P(both), P(both, None)),
        check_vma=False,
    )
```

time: 124 us -> 96.5 us (0.78)
  Pallas kernels: 120 us -> 92.7 us
    pallas_call x1, Pallas kernels: 120 us -> 92.7 us  [shards(): pl.pallas_call(kernel, out_shape=jax.ShapeDtypeStruct((4, 4224), F32), in...]
    slice x0 -> x2, local copies, waits for them, and re-layouts: none -> 2.75 us  [shards(): return (out[:, 4096], out[:, :4096].astype(BF16))]
    unnamed x2 -> x0, local copies, waits for them, and re-layouts: 2.56 us -> none
where the time goes in v2:
time: 96.5 us; the launch traced here: 96.1 us
  Pallas kernels  92.7 us (96%)
  local copies, waits for them, and re-layouts  2.75 us (3%)
    pallas_call x1, Pallas kernels, shards(): pl.pallas_call(kernel, out_shape=jax.ShapeDtypeStruct((4, 4224), F32), in...  92.7 us
    slice x2, local copies, waits for them, and re-layouts, shards(): return (out[:, 4096], out[:, :4096].astype(BF16))  2.75 us

profile of v2, /device:TPU:0, one launch (start us, length us, event | category | flops | bytes accessed | tf_op | source)
XLA Modules:
  0.0 96.1 jit_solution(17489005575864800585)
XLA Ops:
  0.6 92.7 %shard_map.77 = f32[4,4224]{1,0:T(4,128)} custom-call(bf16[4,4096]{1,0:T(4,128)(2,1)} %student_hbm.1, bf16[4,4096]{1,0:T(4,128)(2,1)} %teacher_hbm.1, bf16[4096,1152]{1,0:T(8,128)(2,1)} %shead_hbm.1, bf16[4096,1152]{1,0:T(8,128)(2,1)} %thead_hbm.1, s32[32]{0:T(128)} %count_hbm.1, s32[32]{0:T(128)} %offset_hbm.1), custom_call_target="tpu_custom_call" | custom-call | flops 14495514624 | bytes 19000000 | tf_op jit(solution)/shard_map/pallas_call | solution.py:443
  93.4 1.3 %slice_reduce_fusion = f32[4]{0:T(128)} fusion(f32[4,4224]{1,0:T(4,128)} %shard_map.77), kind=kLoop, calls=%fused_computation.1 | loop fusion | bytes 32 | tf_op jit(solution)/shard_map/slice | solution.py:454
  94.7 1.5 %slice.12 = bf16[4,4096]{1,0:T(4,128)(2,1)} slice(f32[4,4224]{1,0:T(4,128)} %shard_map.77), slice={[0:4], [0:4096]} | slice | bytes 65536 | tf_op jit(solution)/shard_map/slice | solution.py:454

commit v3 on v2

--- a/solution.py
+++ b/solution.py
@@ -8,12 +8,12 @@
 MESH = pl.DeviceIdType.MESH
 F32, BF16 = jnp.float32, jnp.bfloat16
 AXES = ("z", "x", "y")
-GATHER = ((0, 384, ("x", "y", "z")), (384, 384, ("y", "z", "x")), (768, 256, ("z", "x", "y")))
+GATHER = ((0, 256, ("x", "y", "z")), (256, 384, ("y", "z", "x")), (640, 384, ("z", "x", "y")))
 FIRST = ("z", "z", "x", "x", "x", "y", "y", "y")
 THEN = {"z": "x", "x": "y", "y": "x"}
-SEQUENCE = (0, 2, 5, 1, 3, 6, 4, 7)
+SEQUENCE = (2, 5, 0, 3, 6, 1, 4, 7)
 CHUNKS = len(FIRST)
-COPIES = 208
+SENDS, ARRIVALS = 26, 73
 FAR_FIRST = (2, 1, 3)
 VOCAB = 1152
 TILES = VOCAB // 128
@@ -44,17 +44,29 @@
         return device(shifted(axis, delta), core)
 
     sibling = device(me, 1 - core)
-    started = []
-
-    def send(src, dst, to):
-        index = len(started)
-        copy = pltpu.make_async_remote_copy(
-            src_ref=src, dst_ref=dst, send_sem=send_sem.at[index], recv_sem=recv_sem.at[index],
+    sent, used = [], [0, 0]
+
+    def fresh(kind):
+        used[kind] += 1
+        return used[kind] - 1
+
+    def post(src, dst, to, leave, land):
+        pltpu.make_async_remote_copy(
+            src_ref=src, dst_ref=dst, send_sem=send_sem.at[leave], recv_sem=recv_sem.at[land],
             device_id=to, device_id_type=MESH,
-        )
-        copy.start()
-        started.append(copy)
-        return copy
+        ).start()
+
+    def landed(ref, land):
+        pltpu.make_async_remote_copy(
+            src_ref=ref, dst_ref=ref, send_sem=send_sem.at[0], recv_sem=recv_sem.at[land],
+            device_id=sibling, device_id_type=MESH,
+        ).wait_recv()
+
+    def left(ref, leave):
+        pltpu.make_async_remote_copy(
+            src_ref=ref, dst_ref=ref, send_sem=send_sem.at[leave], recv_sem=recv_sem.at[0],
+            device_id=sibling, device_id_type=MESH,
+        ).wait_send()
 
     loads = [
         pltpu.make_async_copy(src, dst, load_sem.at[i])
@@ -79,23 +91,25 @@
     pl.semaphore_wait(barrier, len(friends))
 
     z = me["z"]
-    first = []
-    for delta in (1, 2, 3):
+    leave, land = fresh(0), fresh(1)
+    for delta in FAR_FIRST:
         to = shifted("z", delta)
-        first.append(send(pre_send.at[to["z"]], pre_recv.at[z], device(to, core)))
+        post(pre_send.at[to["z"]], pre_recv.at[z], device(to, core), leave, land)
     pre_recv[z] = pre_send[z]
-    for copy in first:
-        copy.wait_recv()
+    sent.append((pre_send.at[pl.ds(0, 3)], leave))
+    landed(pre_recv.at[pl.ds(0, 3)], land)
     for which in range(2):
         for s in range(4):
             block[4 * s:4 * s + 4, :] = pre_recv[s, 4 * which:4 * which + 4, :]
         rows[which, z, me["x"], me["y"], core] = block[...].astype(BF16)
 
-    def region(part, free, at, c, which=None, half=None):
+    def region(part, free, at, c, which=None, half=None, wide_axis=None, count=3):
         start, width, order = GATHER[part]
         index = [pl.ds(0, 2) if which is None else which]
         for axis in AXES:
-            if axis not in free:
+            if axis == wide_axis:
+                index.append(pl.ds(0, count))
+            elif axis not in free:
                 index.append(at[axis])
             elif half is not None and axis == order[0]:
                 index.append(pl.ds(2 * half, 2))
@@ -108,114 +122,158 @@
     def spread(part, step):
         order = GATHER[part][2]
         here = region(part, order[:step], me, core)
-        return [send(here, here, peer(order[step], delta)) for delta in FAR_FIRST]
-
-    def to_core(part, at, which=None):
+        leave, land = fresh(0), fresh(1)
+        for delta in FAR_FIRST:
+            post(here, here, peer(order[step], delta), leave, land)
+        three = region(part, order[:step], me, core, wide_axis=order[step])
+        sent.append((three, leave))
+        return three, land
+
+    core_leave = [fresh(0) for _ in parts]
+    last_leave = [fresh(0) for _ in parts]
+    last_land = [[{name: fresh(1) for name in ("l0", "r1", "near", "far")} for _ in parts] for _ in range(2)]
+
+    def to_core(part, at, land, which=None):
         here = region(part, GATHER[part][2][:2], at, core, which)
-        return send(here, here, sibling)
+        post(here, here, sibling, core_leave[part], land)
 
     def start_last(which, names):
         for part in parts:
             order = GATHER[part][2]
             for name in names:
                 here = region(part, order[:2], me, core, which, int(name[1]))
-                last[which][part][name] = send(here, here, peer(order[2], 1 if name[0] == "l" else 3))
+                land = last_land[which][part][name if name in ("l0", "r1") else "near"]
+                post(here, here, peer(order[2], 1 if name[0] == "l" else 3), last_leave[part], land)
 
     def pass_on(which):
         for part in parts:
             order = GATHER[part][2]
             for name, delta, half, to in (("l0", 3, 0, 1), ("r1", 1, 1, 3)):
-                last[which][part][name].wait_recv()
                 here = region(part, order[:2], shifted(order[2], delta), core, which, half)
-                last[which][part]["far" + name] = send(here, here, peer(order[2], to))
+                landed(here, last_land[which][part][name])
+                post(here, here, peer(order[2], to), last_leave[part], last_land[which][part]["far"])
+
+    def box_to_core(which, name, deltas):
+        arrivals = []
+        for part in parts:
+            axis, free = GATHER[part][2][2], GATHER[part][2][:2]
+            landed(region(part, free, me, core, which), last_land[which][part][name])
+            land = fresh(1)
+            for delta in deltas:
+                to_core(part, shifted(axis, delta), land, which)
+            arrivals.append((region(part, free, me, core, which, wide_axis=axis, count=len(deltas)), land))
+        return arrivals
 
     def near_to_core(which):
-        copies = []
-        for part in parts:
-            for name, delta in (("l1", 3), ("r0", 1)):
-                last[which][part][name].wait_recv()
-                copies.append(to_core(part, shifted(GATHER[part][2][2], delta), which))
-        return copies
+        return box_to_core(which, "near", (3, 1))
 
     def far_to_core(which):
-        copies = []
-        for part in parts:
-            for name in ("farl0", "farr1"):
-                last[which][part][name].wait_recv()
-            copies.append(to_core(part, shifted(GATHER[part][2][2], 2), which))
-        return copies
-
-    last = [[{} for _ in parts] for _ in range(2)]
+        return box_to_core(which, "far", (2,))
+
     step0 = [spread(part, 0) for part in parts]
     step1 = []
     for part in parts:
-        for copy in step0[part]:
-            copy.wait_recv()
+        landed(*step0[part])
         step1.append(spread(part, 1))
     for part in parts:
-        for copy in step1[part]:
-            copy.wait_recv()
+        landed(*step1[part])
     start_last(0, ("l0", "r1", "l1", "r0"))
     start_last(1, ("l0", "r1"))
-    cores = [[to_core(part, me) for part in parts], []]
+    own_core = []
+    for part in parts:
+        land = fresh(1)
+        to_core(part, me, land)
+        own_core.append((region(part, GATHER[part][2][:2], me, core), land))
+
+    def logits(which, part, deltas, first=False):
+        start, width, order = GATHER[part]
+        axis = order[2]
+        head, out = ((thead, tl), (shead, sl))[which]
+        places = [shifted(axis, delta)[axis] for delta in deltas]
+        cols = slice(start, start + width)
+        if axis == "z":
+            lhs = jnp.concatenate([rows[which, q, :, :, :, :, cols].reshape(512, width) for q in places], axis=1)
+            tops = [pl.multiple_of(q * 1024 + start, 128) for q in places]
+        else:
+            lhs = jnp.concatenate([
+                jnp.concatenate([
+                    (rows[which, q, v, :, :, :, cols] if axis == "x" else rows[which, q, :, v, :, :, cols]).reshape(128, width)
+                    for q in range(4)
+                ], axis=1)
+                for v in places
+            ], axis=0)
+            tops = [q * 1024 + start for q in range(4)]
+        for tile in range(0, TILES, 2):
+            count = min(2, TILES - tile)
+            rhs = jnp.concatenate([head[pl.ds(top, width), tile * 128:(tile + count) * 128] for top in tops], axis=0)
+            total = jnp.dot(lhs, rhs, preferred_element_type=F32)
+            for i in range(count):
+                piece = total[:, i * 128:(i + 1) * 128]
+                if first:
+                    out[tile + i] = piece
+                elif axis == "z":
+                    out[tile + i] += piece
+                else:
+                    for n, v in enumerate(places):
+                        if axis == "x":
+                            at = pl.ds(pl.multiple_of(v * 128, 128), 128)
+                            out[tile + i, at, :] += piece[n * 128:(n + 1) * 128]
+                        else:
+                            for x in range(4):
+                                at = pl.ds(pl.multiple_of(x * 128 + v * 32, 32), 32)
+                                out[tile + i, at, :] += piece[n * 128 + x * 32:n * 128 + x * 32 + 32]
+
+    def add_boxes(which, arrivals, deltas, first=False):
+        for part in parts:
+            landed(*arrivals[part])
+            logits(which, part, deltas, first and part == 0)
+
+    for load in loads[2:]:
+        load.wait()
+    add_boxes(0, own_core, (0,), True)
     pass_on(0)
     start_last(1, ("l1", "r0"))
-    cores[0] += near_to_core(0)
-    cores[0] += far_to_core(0)
-    for copy in cores[0]:
-        copy.wait_recv()
-    loads[4].wait()
-
-    def logits(which, head, out, tile):
-        count = min(2, TILES - tile)
-        total = None
-        for q in range(4):
-            part = jnp.dot(
-                rows[which, q].reshape(512, 1024),
-                head[q * 1024:(q + 1) * 1024, tile * 128:(tile + count) * 128],
-                preferred_element_type=F32,
-            )
-            total = part if total is None else total + part
-        for i in range(count):
-            out[tile + i] = total[:, i * 128:(i + 1) * 128]
-
-    logits(0, thead, tl, 0)
+    for part in parts:
+        logits(1, part, (0,), part == 0)
+    near = near_to_core(0)
     pass_on(1)
-    logits(0, thead, tl, 2)
-    logits(0, thead, tl, 4)
-    cores[1] += near_to_core(1)
-    logits(0, thead, tl, 6)
-    cores[1] += far_to_core(1)
-    logits(0, thead, tl, 8)
-    for copy in cores[1]:
-        copy.wait_recv()
-    for load in (loads[2], loads[3], loads[5]):
-        load.wait()
-    for tile in range(0, TILES, 2):
-        logits(1, shead, sl, tile)
-
-    lane = lax.broadcasted_iota(jnp.int32, (16, 128), 1)
-
-    def terms(g, carry):
-        at = pl.ds(pl.multiple_of(g * 16, 16), 16)
-        pair = pl.ds(offset_ref[g], 16)
-        s = [sl[j, at, :] for j in range(TILES)]
-        t = [tl[j, pair, :] for j in range(TILES)]
-        smax, tmax = s[0], t[0]
+    add_boxes(0, near, (3, 1))
+    far = far_to_core(0)
+    near = near_to_core(1)
+    add_boxes(0, far, (2,))
+    far = far_to_core(1)
+    add_boxes(1, near, (3, 1))
+    add_boxes(1, far, (2,))
+    for part in parts:
+        order = GATHER[part][2]
+        sent.append((region(part, order[:2], me, core, wide_axis=order[2]), last_leave[part]))
+        sent.append((region(part, AXES, me, core), core_leave[part]))
+
+    lane = lax.broadcasted_iota(jnp.int32, (64, 128), 1)
+
+    def terms(b, carry):
+        at = pl.ds(pl.multiple_of(b * 64, 64), 64)
+        pairs = [pl.ds(offset_ref[b * 4 + i], 16) for i in range(4)]
+
+        def paired(j):
+            return jnp.concatenate([tl[j, pair, :] for pair in pairs], axis=0)
+
+        smax, tmax = sl[0, at, :], paired(0)
         for j in range(1, TILES):
-            smax = jnp.maximum(smax, s[j])
-            tmax = jnp.maximum(tmax, t[j])
+            smax = jnp.maximum(smax, sl[j, at, :])
+            tmax = jnp.maximum(tmax, paired(j))
         smax = jnp.max(smax, axis=1, keepdims=True)
         tmax = jnp.max(tmax, axis=1, keepdims=True)
-        ssum = tsum = cross = jnp.zeros((16, 128), F32)
+        ssum = tsum = cross = jnp.zeros((64, 128), F32)
         for j in range(TILES):
-            e = jnp.exp(s[j] - smax)
+            s, t = sl[j, at, :], paired(j)
+            e = jnp.exp(s - smax)
             sl[j, at, :] = e
             ssum = ssum + e
-            e = jnp.exp(t[j] - tmax)
+            e = jnp.exp(t - tmax)
             et[j, at, :] = e
             tsum = tsum + e
-            cross = cross + e * (t[j] - s[j])
+            cross = cross + e * (t - s)
         ssum = jnp.sum(ssum, axis=1, keepdims=True)
         tsum = jnp.sum(tsum, axis=1, keepdims=True)
         cross = jnp.sum(cross, axis=1, keepdims=True)
@@ -223,7 +281,7 @@
         stat[at, :] = tile
         return carry
 
-    lax.fori_loop(0, 32, terms, 0, unroll=4)
+    lax.fori_loop(0, 8, terms, 0)
 
     local = stat[...].T[0:8, :]
     now = local
@@ -231,16 +289,17 @@
     for level, axis in enumerate(("core", "x", "y", "z")):
         st_send[level] = now
         if axis == "core":
-            copies = [send(st_send.at[level], st_recv.at[slot], sibling)]
+            friends = [sibling]
         else:
-            copies = [
-                send(st_send.at[level], st_recv.at[slot + i], peer(axis, delta))
-                for i, delta in enumerate(FAR_FIRST)
-            ]
-        for copy in copies:
-            copy.wait_recv()
-        members = [now] + [st_recv[slot + i] for i in range(len(copies))]
-        slot += len(copies)
+            friends = [peer(axis, delta) for delta in FAR_FIRST]
+        leave, land = fresh(0), fresh(1)
+        for i, friend in enumerate(friends):
+            post(st_send.at[level], st_recv.at[slot + i], friend, leave, land)
+        landing = st_recv.at[pl.ds(slot, len(friends))]
+        sent.append((landing, leave))
+        landed(landing, land)
+        members = [now] + [st_recv[slot + i] for i in range(len(friends))]
+        slot += len(friends)
         smax, tmax = members[0][0:1], members[0][1:2]
         for member in members[1:]:
             smax = jnp.maximum(smax, member[0:1])
@@ -280,6 +339,8 @@
 
     lax.fori_loop(0, 16, prob_diff, 0)
 
+    core_out, first_out = fresh(0), fresh(0)
+
     def grad_matmul(j):
         weights = jnp.concatenate([shead[q * 1024 + j * 128:q * 1024 + (j + 1) * 128, :] for q in range(4)], axis=0)
         out = lax.dot_general(
@@ -289,7 +350,9 @@
             piece = out[:, q * 128:(q + 1) * 128]
             core_send[j, q] = piece[0:256].astype(BF16).reshape(4, 4, 16, 128)
             own[j, q] = piece[256:512].reshape(4, 4, 16, 128)
-        return send(core_send.at[j], core_recv.at[j], sibling)
+        land = fresh(1)
+        post(core_send.at[j], core_recv.at[j], sibling, core_out, land)
+        return land
 
     def pick(ref, j, axis, q):
         index = [slice(None)] * 3
@@ -298,14 +361,14 @@
 
     boxes = {}
 
-    def first_start(j, core_copy):
+    def first_start(j, core_land):
         axis = FIRST[j]
-        core_copy.wait_recv()
-        boxes[j] = []
+        landed(core_recv.at[j], core_land)
+        boxes[j] = fresh(1)
         for i, delta in enumerate(FAR_FIRST):
             q = shifted(axis, delta)[axis]
             stage0[j, i] = (pick(own, j, axis, q) + pick(core_recv, j, axis, q).astype(F32)).astype(BF16)
-            boxes[j].append(send(stage0.at[j, i], recv0.at[j, i], peer(axis, delta)))
+            post(stage0.at[j, i], recv0.at[j, i], peer(axis, delta), first_out, boxes[j])
 
     cur = {"z": curz, "x": curx, "y": cury}
     stage = {"z": stagez, "x": stagex, "y": stagey}
@@ -313,8 +376,7 @@
 
     def first_end(j):
         axis = FIRST[j]
-        for copy in boxes[j]:
-            copy.wait_recv()
+        landed(recv0.at[j], boxes[j])
         total = pick(own, j, axis, me[axis]) + pick(core_recv, j, axis, me[axis]).astype(F32)
         for i in range(3):
             total = total + recv0[j, i].astype(F32)
@@ -323,16 +385,16 @@
             cur[axis][q, place] = total[q] if axis == "z" else total[:, q]
 
     def second_start(axis):
-        copies = []
+        leave, land = fresh(0), fresh(1)
         for i, delta in enumerate(FAR_FIRST):
             q = shifted(THEN[axis], delta)[THEN[axis]]
             stage[axis][i] = cur[axis][q].astype(BF16)
-            copies.append(send(stage[axis].at[i], recv[axis].at[i], peer(THEN[axis], delta)))
-        return copies
-
-    def second_end(axis, copies):
-        for copy in copies:
-            copy.wait_recv()
+            post(stage[axis].at[i], recv[axis].at[i], peer(THEN[axis], delta), leave, land)
+        sent.append((stage[axis], leave))
+        return land
+
+    def second_end(axis, land):
+        landed(recv[axis], land)
         total = cur[axis][me[THEN[axis]]]
         for i in range(3):
             total = total + recv[axis][i].astype(F32)
@@ -341,12 +403,13 @@
     def rows_start(total, fin, got):
         for q in range(4):
             fin[q] = total[:, :, 4 * q:4 * q + 4, :]
-        copies = []
+        leave, land = fresh(0), fresh(1)
         for delta in FAR_FIRST:
             q = shifted("z", delta)["z"]
-            copies.append(send(fin.at[q], got.at[z], peer("z", delta)))
+            post(fin.at[q], got.at[z], peer("z", delta), leave, land)
         got[z] = fin[z]
-        return copies
+        sent.append((fin.at[pl.ds(0, 3)], leave))
+        return got.at[pl.ds(0, 3)], land
 
     waiting = []
     for n, j in enumerate(SEQUENCE):
@@ -355,44 +418,43 @@
             first_start(*waiting.pop(0))
     first_start(*waiting.pop(0))
 
+    sent += [(core_send, core_out), (stage0, first_out)]
     for j in (0, 1):
         first_end(j)
-    zcopies = second_start("z")
+    zland = second_start("z")
     for j in (2, 3, 4):
         first_end(j)
-    xcopies = second_start("x")
+    xland = second_start("x")
     for j in (5, 6, 7):
         first_end(j)
-    ycopies = second_start("y")
-    total = second_end("z", zcopies)
+    yland = second_start("y")
+    total = second_end("z", zland)
     for q in range(4):
         curz2[q] = total[:, q]
-    zcopies = [
-        send(curz2.at[shifted("y", delta)["y"]], recvz2.at[i], peer("y", delta))
-        for i, delta in enumerate(FAR_FIRST)
-    ]
-    xcopies = rows_start(second_end("x", xcopies), finx, gotx)
-    ycopies = rows_start(second_end("y", ycopies), finy, goty)
-    for copy in zcopies:
-        copy.wait_recv()
+    leave, land = fresh(0), fresh(1)
+    for i, delta in enumerate(FAR_FIRST):
+        post(curz2.at[shifted("y", delta)["y"]], recvz2.at[i], peer("y", delta), leave, land)
+    sent.append((recvz2, leave))
+    xrows = rows_start(second_end("x", xland), finx, gotx)
+    yrows = rows_start(second_end("y", yland), finy, goty)
+    landed(recvz2, land)
     total = curz2[me["y"]] + recvz2[0] + recvz2[1] + recvz2[2]
-    zcopies = rows_start(total[None], finz, gotz)
-    for axis, copies, got in (("x", xcopies, gotx), ("y", ycopies, goty)):
-        for copy in copies:
-            copy.wait_recv()
+    zrows = rows_start(total[None], finz, gotz)
+    for axis, arrival, got in (("x", xrows, gotx), ("y", yrows, goty)):
+        landed(*arrival)
         total = got[0] + got[1] + got[2] + got[3]
         for place in range(3):
             for q in range(4):
                 at = q * 1024 + (FIRST.index(axis) + place) * 128
                 out_ref[:, at:at + 128] = total[place, q]
-    for copy in zcopies:
-        copy.wait_recv()
+    landed(*zrows)
     for place in range(2):
         for q in range(4):
             at = q * 1024 + place * 128
             out_ref[:, at:at + 128] = gotz[q, 0, place]
-    for copy in started:
-        copy.wait_send()
+    for ref, leave in sent:
+        left(ref, leave)
+    assert tuple(used) == (SENDS, ARRIVALS), used
 
 
 def shards(student_hidden, teacher_hidden, student_head, teacher_head, group_counts, group_offsets):
@@ -436,8 +498,8 @@
         pltpu.VMEM((4, 1, 2, 4, 128), F32),
         pltpu.VMEM((4, 3, 4, 4, 128), F32),
         pltpu.VMEM((4, 3, 4, 4, 128), F32),
-        pltpu.SemaphoreType.DMA((COPIES,)),
-        pltpu.SemaphoreType.DMA((COPIES,)),
+        pltpu.SemaphoreType.DMA((SENDS,)),
+        pltpu.SemaphoreType.DMA((ARRIVALS,)),
         pltpu.SemaphoreType.DMA((6,)),
     ]
     out = pl.pallas_call(

time: 96.5 us -> 85 us (0.88)
  Pallas kernels: 92.7 us -> 81.5 us
    pallas_call x1, Pallas kernels: 92.7 us -> 81.5 us  [shards(): pl.pallas_call(kernel, out_shape=jax.ShapeDtypeStruct((4, 4224), F32), in...]
where the time goes in v3:
time: 85 us; the launch traced here: 84.9 us
  Pallas kernels  81.5 us (96%)
  local copies, waits for them, and re-layouts  2.75 us (3%)
    pallas_call x1, Pallas kernels, shards(): pl.pallas_call(kernel, out_shape=jax.ShapeDtypeStruct((4, 4224), F32), in...  81.5 us
    slice x2, local copies, waits for them, and re-layouts, shards(): return (out[:, 4096], out[:, :4096].astype(BF16))  2.75 us

profile of v3, /device:TPU:0, one launch (start us, length us, event | category | flops | bytes accessed | tf_op | source)
XLA Modules:
  0.0 84.9 jit_solution(2724071402699700424)
XLA Ops:
  0.6 81.5 %shard_map.77 = f32[4,4224]{1,0:T(4,128)} custom-call(bf16[4,4096]{1,0:T(4,128)(2,1)} %student_hbm.1, bf16[4,4096]{1,0:T(4,128)(2,1)} %teacher_hbm.1, bf16[4096,1152]{1,0:T(8,128)(2,1)} %shead_hbm.1, bf16[4096,1152]{1,0:T(8,128)(2,1)} %thead_hbm.1, s32[32]{0:T(128)} %count_hbm.1, s32[32]{0:T(128)} %offset_hbm.1), custom_call_target="tpu_custom_call" | custom-call | flops 14495514624 | bytes 19000000 | tf_op jit(solution)/shard_map/pallas_call | solution.py:505
  82.1 1.3 %slice_reduce_fusion = f32[4]{0:T(128)} fusion(f32[4,4224]{1,0:T(4,128)} %shard_map.77), kind=kLoop, calls=%fused_computation.1 | loop fusion | bytes 32 | tf_op jit(solution)/shard_map/slice | solution.py:516
  83.4 1.5 %slice.12 = bf16[4,4096]{1,0:T(4,128)(2,1)} slice(f32[4,4224]{1,0:T(4,128)} %shard_map.77), slice={[0:4], [0:4096]} | slice | bytes 65536 | tf_op jit(solution)/shard_map/slice | solution.py:516

commit v4 on v3

--- a/solution.py
+++ b/solution.py
@@ -11,9 +11,11 @@
 GATHER = ((0, 256, ("x", "y", "z")), (256, 384, ("y", "z", "x")), (640, 384, ("z", "x", "y")))
 FIRST = ("z", "z", "x", "x", "x", "y", "y", "y")
 THEN = {"z": "x", "x": "y", "y": "x"}
-SEQUENCE = (2, 5, 0, 3, 6, 1, 4, 7)
+SEQUENCE = (2, 5, 0, 1, 3, 6, 4, 7)
+LAG = 2
+PLANE = sorted(((a, b) for a in range(4) for b in range(4) if a or b), key=lambda d: -sum(min(e, 4 - e) for e in d))
 CHUNKS = len(FIRST)
-SENDS, ARRIVALS = 26, 73
+SENDS, ARRIVALS = 24, 71
 FAR_FIRST = (2, 1, 3)
 VOCAB = 1152
 TILES = VOCAB // 128
@@ -24,7 +26,7 @@
     out_ref,
     student_ref, teacher_ref, count_ref, offset_ref,
     shead, thead, rows, sl, tl, et, pd,
-    pre_send, pre_recv, block, stat, st_send, st_recv,
+    pre_send, pre_recv, pack, block, stat, st_send, st_recv,
     core_send, core_recv, own, stage0, recv0,
     curz, curx, cury, stagez, stagex, stagey, recvz, recvx, recvy, curz2, recvz2,
     finz, finx, finy, gotz, gotx, goty,
@@ -86,8 +88,11 @@
     for load in loads[:2]:
         load.wait()
     for q in range(4):
-        pre_send[q, 0:4, :] = teacher_ref[:, q * 1024:(q + 1) * 1024].astype(F32)
-        pre_send[q, 4:8, :] = student_ref[:, q * 1024:(q + 1) * 1024].astype(F32)
+        for h in range(2):
+            at = slice(q * 1024 + h * 512, q * 1024 + h * 512 + 512)
+            pack[q, 4 * h:4 * h + 4, :] = teacher_ref[:, at].astype(F32)
+            pack[q, 8 + 4 * h:12 + 4 * h, :] = student_ref[:, at].astype(F32)
+    pre_send[...] = pack[...].astype(BF16)
     pl.semaphore_wait(barrier, len(friends))
 
     z = me["z"]
@@ -98,9 +103,12 @@
     pre_recv[z] = pre_send[z]
     sent.append((pre_send.at[pl.ds(0, 3)], leave))
     landed(pre_recv.at[pl.ds(0, 3)], land)
+    pack[...] = pre_recv[...].astype(F32)
     for which in range(2):
         for s in range(4):
-            block[4 * s:4 * s + 4, :] = pre_recv[s, 4 * which:4 * which + 4, :]
+            for h in range(2):
+                top = 8 * which + 4 * h
+                block[4 * s:4 * s + 4, h * 512:h * 512 + 512] = pack[s, top:top + 4, :]
         rows[which, z, me["x"], me["y"], core] = block[...].astype(BF16)
 
     def region(part, free, at, c, which=None, half=None, wide_axis=None, count=3):
@@ -286,12 +294,12 @@
     local = stat[...].T[0:8, :]
     now = local
     slot = 0
-    for level, axis in enumerate(("core", "x", "y", "z")):
+    for level in range(2):
         st_send[level] = now
-        if axis == "core":
-            friends = [sibling]
+        if level == 0:
+            friends = [device(shifted("x", delta), c) for delta in FAR_FIRST for c in (1 - core, core)] + [sibling]
         else:
-            friends = [peer(axis, delta) for delta in FAR_FIRST]
+            friends = [device({**shifted("y", a), "z": shifted("z", b)["z"]}, core) for a, b in PLANE]
         leave, land = fresh(0), fresh(1)
         for i, friend in enumerate(friends):
             post(st_send.at[level], st_recv.at[slot + i], friend, leave, land)
@@ -337,7 +345,7 @@
                 pd[half, pair, :, j * 128:(j + 1) * 128] = (sl[j, at, :] * a - et[j, at, :] * b).astype(BF16)
         return carry
 
-    lax.fori_loop(0, 16, prob_diff, 0)
+    lax.fori_loop(0, 16, prob_diff, 0, unroll=4)
 
     core_out, first_out = fresh(0), fresh(0)
 
@@ -350,10 +358,6 @@
             piece = out[:, q * 128:(q + 1) * 128]
             core_send[j, q] = piece[0:256].astype(BF16).reshape(4, 4, 16, 128)
             own[j, q] = piece[256:512].reshape(4, 4, 16, 128)
-        land = fresh(1)
-        post(core_send.at[j], core_recv.at[j], sibling, core_out, land)
-        return land
-
     def pick(ref, j, axis, q):
         index = [slice(None)] * 3
         index[AXES.index(axis)] = q
@@ -361,14 +365,17 @@
 
     boxes = {}
 
-    def first_start(j, core_land):
+    def first_stage(j, core_land):
         axis = FIRST[j]
         landed(core_recv.at[j], core_land)
-        boxes[j] = fresh(1)
         for i, delta in enumerate(FAR_FIRST):
             q = shifted(axis, delta)[axis]
             stage0[j, i] = (pick(own, j, axis, q) + pick(core_recv, j, axis, q).astype(F32)).astype(BF16)
-            post(stage0.at[j, i], recv0.at[j, i], peer(axis, delta), first_out, boxes[j])
+
+    def first_start(j):
+        boxes[j] = fresh(1)
+        for i, delta in enumerate(FAR_FIRST):
+            post(stage0.at[j, i], recv0.at[j, i], peer(FIRST[j], delta), first_out, boxes[j])
 
     cur = {"z": curz, "x": curx, "y": cury}
     stage = {"z": stagez, "x": stagex, "y": stagey}
@@ -411,22 +418,25 @@
         sent.append((fin.at[pl.ds(0, 3)], leave))
         return got.at[pl.ds(0, 3)], land
 
-    waiting = []
-    for n, j in enumerate(SEQUENCE):
-        waiting.append((j, grad_matmul(j)))
-        if n >= 1:
-            first_start(*waiting.pop(0))
-    first_start(*waiting.pop(0))
+    core_land = {}
+    for n in range(CHUNKS + LAG):
+        if n < CHUNKS:
+            j = SEQUENCE[n]
+            grad_matmul(j)
+            core_land[j] = fresh(1)
+            post(core_send.at[j], core_recv.at[j], sibling, core_out, core_land[j])
+        if n >= LAG:
+            first_stage(SEQUENCE[n - LAG], core_land[SEQUENCE[n - LAG]])
+            first_start(SEQUENCE[n - LAG])
 
     sent += [(core_send, core_out), (stage0, first_out)]
     for j in (0, 1):
         first_end(j)
     zland = second_start("z")
-    for j in (2, 3, 4):
+    for j in (2, 5, 3, 6, 4):
         first_end(j)
     xland = second_start("x")
-    for j in (5, 6, 7):
-        first_end(j)
+    first_end(7)
     yland = second_start("y")
     total = second_end("z", zland)
     for q in range(4):
@@ -470,12 +480,13 @@
         pltpu.VMEM((2, 4, 4, 4, 2, 16, 1024), BF16),
         table, table, table,
         pltpu.VMEM((2, 16, 16, VOCAB), BF16),
-        pltpu.VMEM((4, 8, 1024), F32),
-        pltpu.VMEM((4, 8, 1024), F32),
+        pltpu.VMEM((4, 16, 512), BF16),
+        pltpu.VMEM((4, 16, 512), BF16),
+        pltpu.VMEM((4, 16, 512), F32),
         pltpu.VMEM((16, 1024), F32),
         pltpu.VMEM((512, 128), F32),
-        pltpu.VMEM((4, 8, 512), F32),
-        pltpu.VMEM((10, 8, 512), F32),
+        pltpu.VMEM((2, 8, 512), F32),
+        pltpu.VMEM((22, 8, 512), F32),
         pltpu.VMEM((CHUNKS, 4, 4, 4, 16, 128), BF16),
         pltpu.VMEM((CHUNKS, 4, 4, 4, 16, 128), BF16),
         pltpu.VMEM((CHUNKS, 4, 4, 4, 16, 128), F32),

time: 85 us -> 81.2 us (0.955)
  Pallas kernels: 81.5 us -> 77.6 us
    pallas_call x1, Pallas kernels: 81.5 us -> 77.6 us  [shards(): pl.pallas_call(kernel, out_shape=jax.ShapeDtypeStruct((4, 4224), F32), in...]
where the time goes in v4:
time: 81.2 us; the launch traced here: 81 us
  Pallas kernels  77.6 us (96%)
  local copies, waits for them, and re-layouts  2.75 us (3%)
    pallas_call x1, Pallas kernels, shards(): pl.pallas_call(kernel, out_shape=jax.ShapeDtypeStruct((4, 4224), F32), in...  77.6 us
    slice x2, local copies, waits for them, and re-layouts, shards(): return (out[:, 4096], out[:, :4096].astype(BF16))  2.75 us

profile of v4, /device:TPU:0, one launch (start us, length us, event | category | flops | bytes accessed | tf_op | source)
XLA Modules:
  0.0 81.0 jit_solution(8186294953628180471)
XLA Ops:
  0.6 77.6 %shard_map.77 = f32[4,4224]{1,0:T(4,128)} custom-call(bf16[4,4096]{1,0:T(4,128)(2,1)} %student_hbm.1, bf16[4,4096]{1,0:T(4,128)(2,1)} %teacher_hbm.1, bf16[4096,1152]{1,0:T(8,128)(2,1)} %shead_hbm.1, bf16[4096,1152]{1,0:T(8,128)(2,1)} %thead_hbm.1, s32[32]{0:T(128)} %count_hbm.1, s32[32]{0:T(128)} %offset_hbm.1), custom_call_target="tpu_custom_call" | custom-call | flops 14495514624 | bytes 19000000 | tf_op jit(solution)/shard_map/pallas_call | solution.py:516
  78.3 1.3 %slice_reduce_fusion = f32[4]{0:T(128)} fusion(f32[4,4224]{1,0:T(4,128)} %shard_map.77), kind=kLoop, calls=%fused_computation.1 | loop fusion | bytes 32 | tf_op jit(solution)/shard_map/slice | solution.py:527
  79.6 1.5 %slice.12 = bf16[4,4096]{1,0:T(4,128)(2,1)} slice(f32[4,4224]{1,0:T(4,128)} %shard_map.77), slice={[0:4], [0:4096]} | slice | bytes 65536 | tf_op jit(solution)/shard_map/slice | solution.py:527

commit v5 on v4

--- a/solution.py
+++ b/solution.py
@@ -244,12 +244,23 @@
     for part in parts:
         logits(1, part, (0,), part == 0)
     near = near_to_core(0)
+    landed(*near[0])
+    logits(0, 0, (3, 1))
     pass_on(1)
-    add_boxes(0, near, (3, 1))
+    landed(*near[1])
+    logits(0, 1, (3, 1))
     far = far_to_core(0)
-    near = near_to_core(1)
-    add_boxes(0, far, (2,))
-    far = far_to_core(1)
+    landed(*near[2])
+    logits(0, 2, (3, 1))
+    near1 = near_to_core(1)
+    landed(*far[0])
+    logits(0, 0, (2,))
+    landed(*far[1])
+    logits(0, 1, (2,))
+    landed(*far[2])
+    logits(0, 2, (2,))
+    far1 = far_to_core(1)
+    near, far = near1, far1
     add_boxes(1, near, (3, 1))
     add_boxes(1, far, (2,))
     for part in parts:
@@ -289,7 +300,7 @@
         stat[at, :] = tile
         return carry
 
-    lax.fori_loop(0, 8, terms, 0)
+    lax.fori_loop(0, 8, terms, 0, unroll=2)
 
     local = stat[...].T[0:8, :]
     now = local

time: 81.2 us -> 79.8 us (0.983)
  Pallas kernels: 77.6 us -> 76.3 us
    pallas_call x1, Pallas kernels: 77.6 us -> 76.3 us  [shards(): pl.pallas_call(kernel, out_shape=jax.ShapeDtypeStruct((4, 4224), F32), in...]
where the time goes in v5:
time: 79.8 us; the launch traced here: 79.6 us
  Pallas kernels  76.3 us (96%)
  local copies, waits for them, and re-layouts  2.75 us (3%)
    pallas_call x1, Pallas kernels, shards(): pl.pallas_call(kernel, out_shape=jax.ShapeDtypeStruct((4, 4224), F32), in...  76.3 us
    slice x2, local copies, waits for them, and re-layouts, shards(): return (out[:, 4096], out[:, :4096].astype(BF16))  2.75 us

profile of v5, /device:TPU:0, one launch (start us, length us, event | category | flops | bytes accessed | tf_op | source)
XLA Modules:
  0.0 79.6 jit_solution(11437403286019850422)
XLA Ops:
  0.6 76.3 %shard_map.77 = f32[4,4224]{1,0:T(4,128)} custom-call(bf16[4,4096]{1,0:T(4,128)(2,1)} %student_hbm.1, bf16[4,4096]{1,0:T(4,128)(2,1)} %teacher_hbm.1, bf16[4096,1152]{1,0:T(8,128)(2,1)} %shead_hbm.1, bf16[4096,1152]{1,0:T(8,128)(2,1)} %thead_hbm.1, s32[32]{0:T(128)} %count_hbm.1, s32[32]{0:T(128)} %offset_hbm.1), custom_call_target="tpu_custom_call" | custom-call | flops 14495514624 | bytes 19000000 | tf_op jit(solution)/shard_map/pallas_call | solution.py:527
  76.9 1.3 %slice_reduce_fusion = f32[4]{0:T(128)} fusion(f32[4,4224]{1,0:T(4,128)} %shard_map.77), kind=kLoop, calls=%fused_computation.1 | loop fusion | bytes 32 | tf_op jit(solution)/shard_map/slice | solution.py:538
  78.2 1.5 %slice.12 = bf16[4,4096]{1,0:T(4,128)(2,1)} slice(f32[4,4224]{1,0:T(4,128)} %shard_map.77), slice={[0:4], [0:4096]} | slice | bytes 65536 | tf_op jit(solution)/shard_map/slice | solution.py:538

commit v6 on v5

--- a/solution.py
+++ b/solution.py
@@ -15,7 +15,7 @@
 LAG = 2
 PLANE = sorted(((a, b) for a in range(4) for b in range(4) if a or b), key=lambda d: -sum(min(e, 4 - e) for e in d))
 CHUNKS = len(FIRST)
-SENDS, ARRIVALS = 24, 71
+SENDS, ARRIVALS = 26, 73
 FAR_FIRST = (2, 1, 3)
 VOCAB = 1152
 TILES = VOCAB // 128
@@ -186,13 +186,13 @@
     for part in parts:
         landed(*step1[part])
     start_last(0, ("l0", "r1", "l1", "r0"))
-    start_last(1, ("l0", "r1"))
     own_core = []
     for part in parts:
         land = fresh(1)
         to_core(part, me, land)
         own_core.append((region(part, GATHER[part][2][:2], me, core), land))
 
+    start_last(1, ("l0", "r1"))
     def logits(which, part, deltas, first=False):
         start, width, order = GATHER[part]
         axis = order[2]
@@ -402,17 +402,19 @@
         for q in range(4):
             cur[axis][q, place] = total[q] if axis == "z" else total[:, q]
 
-    def second_start(axis):
+    def second_start(axis, low, count):
         leave, land = fresh(0), fresh(1)
+        tiles = pl.ds(low, count)
         for i, delta in enumerate(FAR_FIRST):
             q = shifted(THEN[axis], delta)[THEN[axis]]
-            stage[axis][i] = cur[axis][q].astype(BF16)
-            post(stage[axis].at[i], recv[axis].at[i], peer(THEN[axis], delta), leave, land)
-        sent.append((stage[axis], leave))
-        return land
-
-    def second_end(axis, land):
-        landed(recv[axis], land)
+            stage[axis][i, tiles] = cur[axis][q, tiles].astype(BF16)
+            post(stage[axis].at[i, tiles], recv[axis].at[i, tiles], peer(THEN[axis], delta), leave, land)
+        sent.append((stage[axis].at[pl.ds(0, 3), tiles], leave))
+        return recv[axis].at[pl.ds(0, 3), tiles], land
+
+    def second_end(axis, arrivals):
+        for arrival in arrivals:
+            landed(*arrival)
         total = cur[axis][me[THEN[axis]]]
         for i in range(3):
             total = total + recv[axis][i].astype(F32)
@@ -443,12 +445,17 @@
     sent += [(core_send, core_out), (stage0, first_out)]
     for j in (0, 1):
         first_end(j)
-    zland = second_start("z")
-    for j in (2, 5, 3, 6, 4):
+    zland = [second_start("z", 0, 2)]
+    for j in (2, 3):
         first_end(j)
-    xland = second_start("x")
+    xland = [second_start("x", 0, 2)]
+    for j in (5, 6):
+        first_end(j)
+    yland = [second_start("y", 0, 2)]
+    first_end(4)
+    xland.append(second_start("x", 2, 1))
     first_end(7)
-    yland = second_start("y")
+    yland.append(second_start("y", 2, 1))
     total = second_end("z", zland)
     for q in range(4):
         curz2[q] = total[:, q]

time: 79.8 us -> 79.9 us (level)
  no operation moved by 1% of the time
where the time goes in v6:
time: 79.9 us; the launch traced here: 79.8 us
  Pallas kernels  76.4 us (96%)
  local copies, waits for them, and re-layouts  2.75 us (3%)
    pallas_call x1, Pallas kernels, shards(): pl.pallas_call(kernel, out_shape=jax.ShapeDtypeStruct((4, 4224), F32), in...  76.4 us
    slice x2, local copies, waits for them, and re-layouts, shards(): return (out[:, 4096], out[:, :4096].astype(BF16))  2.75 us

profile of v6, /device:TPU:0, one launch (start us, length us, event | category | flops | bytes accessed | tf_op | source)
XLA Modules:
  0.0 79.8 jit_solution(568952101347430376)
XLA Ops:
  0.6 76.4 %shard_map.77 = f32[4,4224]{1,0:T(4,128)} custom-call(bf16[4,4096]{1,0:T(4,128)(2,1)} %student_hbm.1, bf16[4,4096]{1,0:T(4,128)(2,1)} %teacher_hbm.1, bf16[4096,1152]{1,0:T(8,128)(2,1)} %shead_hbm.1, bf16[4096,1152]{1,0:T(8,128)(2,1)} %thead_hbm.1, s32[32]{0:T(128)} %count_hbm.1, s32[32]{0:T(128)} %offset_hbm.1), custom_call_target="tpu_custom_call" | custom-call | flops 14495514624 | bytes 19000000 | tf_op jit(solution)/shard_map/pallas_call | solution.py:534
  77.0 1.3 %slice_reduce_fusion = f32[4]{0:T(128)} fusion(f32[4,4224]{1,0:T(4,128)} %shard_map.77), kind=kLoop, calls=%fused_computation.1 | loop fusion | bytes 32 | tf_op jit(solution)/shard_map/slice | solution.py:545
  78.3 1.5 %slice.12 = bf16[4,4096]{1,0:T(4,128)(2,1)} slice(f32[4,4224]{1,0:T(4,128)} %shard_map.77), slice={[0:4], [0:4096]} | slice | bytes 65536 | tf_op jit(solution)/shard_map/slice | solution.py:545
